TPU v7x, 128 devices: a whole 4x4x4 slice. The times are simulated.
128 devices in a mesh: tm: 16 (over y_lo, z, core), space: 8 (over x, y_hi).
Axes of the slice: x: 4, y: 4 (y_hi: 2, y_lo: 2; y = y_hi * 2 + y_lo), z: 4, core: 2. Of those that a mesh axis runs over, the one named last changes fastest.
Arguments:
- initial_temp: float32 [128, 32, 256], P('space'), may hold values from -6 to 6
- region_labels: int32 [32, 8, 64], P('space'), may hold values from 0 to 5
- region_rate: float32 [6], replicated, may hold values from 0.5 to 8
- heat_rate: float32 [16, 6], replicated, may hold values from 0.1 to 2
Outputs:
- slice_end: float32 [16, 128, 32, 256], P('tm', 'space')
All inputs are finite; a program needn't handle non-finite values.
Results may differ from a plain program's by a relative error of at most 0.0001.
Values sent between devices are 32-bit elements; how exact they have to be, the bound alone decides.
No kernel may reach another device: no remote copies, remote signals or barrier semaphores. Data moves between devices by JAX's collectives and lax.ppermute only.
A program may use at most 128 MiB of HBM per device.

v0:
```python
import jax
import jax.numpy as jnp
from jax import lax
from jax.sharding import PartitionSpec as P

FINE_STEPS = 2
SWEEPS = 8
C_SWEEPS = 4
PARA_ITERS = 2


def with_halo(array, sides, width):
    for axis, dim in sides:
        peers, length = (lax.axis_size(axis), array.shape[dim])
        up = [(i, (i + 1) % peers) for i in range(peers - 1)]
        down = [(j, i) for i, j in up]
        last = lax.slice_in_dim(array, length - width, length, axis=dim)
        initial = lax.slice_in_dim(array, 0, width, axis=dim)
        before = lax.ppermute(last, axis, up)
        after = lax.ppermute(initial, axis, down)
        array = jnp.concatenate([before, array, after], axis=dim)
    return array


def shifted(array, axis, by):
    peers = lax.axis_size(axis)
    pairs = [(i, i + by) for i in range(peers) if 0 <= i + by < peers]
    return lax.ppermute(array, axis, pairs)


def neighbours(field):
    padded = jnp.pad(field, 1)
    total = padded[2:, 1:-1, 1:-1] + padded[:-2, 1:-1, 1:-1]
    total = total + padded[1:-1, 2:, 1:-1] + padded[1:-1, :-2, 1:-1]
    total = total + padded[1:-1, 1:-1, 2:] + padded[1:-1, 1:-1, :-2]
    return total


def expand(block):
    sx, sy, sz = block.shape
    wide = jnp.broadcast_to(block[:, None, :, None, :, None], (sx, 4, sy, 4, sz, 4))
    return wide.reshape((4 * sx, 4 * sy, 4 * sz))


def restrict(field):
    sx, sy, sz = field.shape
    split = field.reshape((sx // 4, 4, sy // 4, 4, sz // 4, 4))
    return jnp.mean(split, axis=(1, 3, 5))


def lookup(labels, table):
    total = jnp.zeros(labels.shape, jnp.float32)
    for region in range(table.shape[0]):
        total = total + jnp.where(labels == region, table[region], jnp.float32(0.0))
    return total


def on_device(initial_temp, region_labels, region_rate, heat_rate):
    slice_index = lax.axis_index("tm")
    slice_count = lax.axis_size("tm")
    heat_row = lax.dynamic_index_in_dim(heat_rate, slice_index, 0, keepdims=False)
    rate_block = lookup(region_labels, region_rate)
    rate_fine = expand(rate_block)
    inv_fine = 1.0 / (1.0 + 6.0 * rate_fine)
    weight_fine = rate_fine * inv_fine
    source_fine = expand(lookup(region_labels, heat_row))
    rim_width = 2
    fine_coeffs = with_halo(
        jnp.stack([inv_fine, weight_fine, source_fine]), (("space", 1),), rim_width
    )

    def fine_halo(field):
        return with_halo(field, (("space", 0),), rim_width)

    rate_coarse = FINE_STEPS * rate_block / 16.0
    inv_coarse = 1.0 / (1.0 + 6.0 * rate_coarse)
    weight_coarse = rate_coarse * inv_coarse
    source_coarse = FINE_STEPS * lookup(region_labels, heat_row)
    coarse_coeffs = with_halo(
        jnp.stack([inv_coarse, weight_coarse, source_coarse]), (("space", 1),), C_SWEEPS
    )
    start = restrict(initial_temp)

    def coarse_step(coarse):
        field_ext = with_halo(coarse, (("space", 0),), C_SWEEPS)
        scaled = (field_ext + coarse_coeffs[2]) * coarse_coeffs[0]
        for sweep_index in range(C_SWEEPS):
            field_ext = scaled + coarse_coeffs[1] * neighbours(field_ext)
        return field_ext[C_SWEEPS:-C_SWEEPS]

    def run_chain(delta):
        offset = jnp.zeros_like(start) if delta is None else delta

        def turn(turn_index, incoming):
            moved = shifted(coarse_step(incoming) + offset, "tm", 1)
            return jnp.where(slice_index == 0, start, moved)

        arrived = lax.fori_loop(0, slice_count - 1, turn, start)
        return (arrived, coarse_step(arrived))

    own_start, previous_end = run_chain(None)
    state = jnp.where(slice_index == 0, initial_temp, expand(own_start))
    result = state
    for iteration in range(PARA_ITERS):
        fine_state = state
        for fine_step in range(FINE_STEPS):
            fine_field_ext = fine_halo(fine_state)
            fine_scaled = (fine_field_ext + fine_coeffs[2]) * fine_coeffs[0]
            for block_index in range(SWEEPS // rim_width):
                if block_index > 0:
                    fine_field_ext = fine_halo(fine_state)
                for fine_sweep_index in range(rim_width):
                    fine_field_ext = fine_scaled + fine_coeffs[1] * neighbours(fine_field_ext)
                fine_state = fine_field_ext[rim_width:-rim_width]
        delta = restrict(fine_state) - previous_end
        own_start, own_end = run_chain(delta)
        correction = own_end - previous_end
        previous_end = own_end
        if iteration + 1 < PARA_ITERS:
            moved = shifted(fine_state + expand(correction), "tm", 1)
            state = jnp.where(slice_index == 0, initial_temp, moved)
        else:
            result = fine_state + expand(correction)
    return result[None]


def solution(mesh):
    return jax.shard_map(
        on_device,
        mesh=mesh,
        in_specs=(P("space", None, None), P("space", None, None), P(), P()),
        out_specs=P("tm", "space", None, None),
        check_vma=False,
    )
```

profile of v0, /device:TPU:8, one launch (start us, length us, event | category | flops | bytes accessed | tf_op | source)
XLA Modules:
  0.0 1263.4 jit_solution(4654690050117450778)
XLA Ops:
  11.9 6.1 collective-permute-start.9
  17.9 8.1 broadcast_in_dim.112
  26.0 15.0 %stack_reshape.3 = f32[1,16,32,256]{3,2,1,0:T(8,128)S(1)} reshape(f32[4,4,8,4,64,4]{5,4,3,2,1,0:T(8,128)} %broadcast_in_dim.112) | data formatting | bytes 1048576 | tf_op jit(solution)/shard_map/stack;reshape | solution.py:69
  41.0 8.1 broadcast_in_dim.111
  49.1 15.0 %reshape.69 = f32[1,16,32,256]{3,2,1,0:T(8,128)S(1)} reshape(f32[4,4,8,4,64,4]{5,4,3,2,1,0:T(8,128)} %broadcast_in_dim.111) | data formatting | bytes 1048576 | tf_op jit(solution)/shard_map/reshape | solution.py:42
  70.8 18.7 %reshape.67 = f32[4,4,8,4,64,4]{5,4,3,2,1,0:T(8,128)} reshape(f32[16,32,256]{2,1,0:T(8,128)S(1)} %copy-done.2) | data formatting | bytes 1048576 | tf_op jit(solution)/shard_map/reshape | solution.py:47
  89.5 7.0 reduce_sum.27
  96.6 275.5 %while.36 = (s32[]{:T(128)}, f32[4,8,64]{2,1,0:T(8,128)S(1)}, pred[]{:T(512)}, f32[3,12,8,64]{3,2,1,0:T(8,128)S(1)}, f32[4,8,64]{2,1,0:T(8,128)S(1)}, /*index=5*/s32[]{:T(128)}) while((s32[]{:T(128)}, f32[4,8,64]{2,1,0:T(8,128)S(1)}, pred[]{:T(512)}, f32[3,12,8,64]{3,2,1,0:T(8,128)S(1)}, f32[4,8,64]{2,1,0:T(8,128)S(1)}, ...), condition=%wide.region_2.3_spmd, body=%wide.region_1.2_spmd.sunk | while | flops 161794 | bytes 819390 | solution.py:98
  375.5 8.1 broadcast_in_dim.110
  383.6 15.0 %reshape.68 = f32[16,32,256]{2,1,0:T(8,128)S(1)} reshape(f32[4,4,8,4,64,4]{5,4,3,2,1,0:T(8,128)} %broadcast_in_dim.110) | data formatting | bytes 1048576 | tf_op jit(solution)/shard_map/reshape | solution.py:42
  455.8 6.1 collective-permute-done.22
  467.7 6.2 collective-permute-done.24
  501.1 18.7 %reshape.70 = f32[4,4,8,4,64,4]{5,4,3,2,1,0:T(8,128)} reshape(f32[16,32,256]{2,1,0:T(8,128)S(1)} %slice_add_fusion.80) | data formatting | bytes 1048576 | tf_op jit(solution)/shard_map/reshape | solution.py:47
  519.7 7.6 reduce_sum.28
  528.7 263.4 %while.37 = (s32[]{:T(128)}, f32[4,8,64]{2,1,0:T(8,128)S(1)}, pred[]{:T(512)}, f32[3,12,8,64]{3,2,1,0:T(8,128)S(1)}, f32[4,8,64]{2,1,0:T(8,128)S(1)}, /*index=5*/f32[4,8,64]{2,1,0:T(8,128)S(1)}, s32[]{:T(128)}) while((s32[]{:T(128)}, f32[4,8,64]{2,1,0:T(8,128)S(1)}, pred[]{:T(512)}, f32[3,12,8,64]{3,2,1,0:T(8,128)S(1)}, ...), condition=%wide.region_5.6_spmd, body=%wide.region_4.5_spmd.sunk | while | flops 163842 | bytes 827590 | solution.py:98
  802.4 8.0 broadcast_in_dim.113
  810.5 15.7 %reshape.71 = f32[16,32,256]{2,1,0:T(8,128)} reshape(f32[4,4,8,4,64,4]{5,4,3,2,1,0:T(8,128)} %broadcast_in_dim.113) | data formatting | bytes 1048576 | tf_op jit(solution)/shard_map/reshape | solution.py:42
  829.2 12.1 collective-permute-done.33
  844.7 6.1 collective-permute-done.35
  939.6 18.7 %reshape.72 = f32[4,4,8,4,64,4]{5,4,3,2,1,0:T(8,128)} reshape(f32[16,32,256]{2,1,0:T(8,128)S(1)} %slice_add_fusion.75) | data formatting | bytes 1048576 | tf_op jit(solution)/shard_map/reshape | solution.py:47
  958.3 7.0 reduce_sum.29
  965.4 263.2 %while.38 = (s32[]{:T(128)}, f32[4,8,64]{2,1,0:T(8,128)S(1)}, pred[]{:T(512)}, f32[3,12,8,64]{3,2,1,0:T(8,128)S(1)}, f32[4,8,64]{2,1,0:T(8,128)S(1)}, /*index=5*/f32[4,8,64]{2,1,0:T(8,128)S(1)}, s32[]{:T(128)}) while((s32[]{:T(128)}, f32[4,8,64]{2,1,0:T(8,128)S(1)}, pred[]{:T(512)}, f32[3,12,8,64]{3,2,1,0:T(8,128)S(1)}, ...), condition=%wide.region_8.9_spmd, body=%wide.region_7.8_spmd.sunk | while | flops 163842 | bytes 827590 | solution.py:98
  1239.0 8.1 broadcast_in_dim.114
  1247.0 15.0 %reshape.73 = f32[16,32,256]{2,1,0:T(8,128)S(1)} reshape(f32[4,4,8,4,64,4]{5,4,3,2,1,0:T(8,128)} %broadcast_in_dim.114) | data formatting | bytes 1048576 | tf_op jit(solution)/shard_map/reshape | solution.py:42
  (947 shorter events, 1028.6 us)
Async XLA Ops:
  10.6 86.0 %collective-permute-start.10 = (f32[3,4,8,64]{3,2,1,0:T(8,128)S(1)}, f32[3,4,8,64]{3,2,1,0:T(8,128)S(1)}, u32[]{:S(2)}, u32[]{:S(2)}) collective-permute-start(f32[3,4,8,64]{3,2,1,0:T(8,128)S(1)} %pad_maximum_fusion.9), channel_id=1, source_target_pairs={{1,0},{2,1},{3,2},{4,3},{5,4},{6,5},{7,6},{9,8},{10,9},{11,10},{12... | collective-permute-start | bytes 73736 | tf_op jit(solution)/shard_map/ppermute | solution.py:20
  11.9 84.7 %collective-permute-start.9 = (f32[3,4,8,64]{3,2,1,0:T(8,128)S(1)}, f32[3,4,8,64]{3,2,1,0:T(8,128)S(1)}, u32[]{:S(2)}, u32[]{:S(2)}) collective-permute-start(f32[3,4,8,64]{3,2,1,0:T(8,128)S(1)} %pad_maximum_fusion.9), channel_id=1, source_target_pairs={{0,1},{1,2},{2,3},{3,4},{4,5},{5,6},{6,7},{8,9},{9,10},{10,11},{11... | collective-permute-start | bytes 73736 | tf_op jit(solution)/shard_map/ppermute | solution.py:19
  64.3 344.2 %collective-permute-start.13 = (f32[3,2,32,256]{3,2,1,0:T(8,128)S(1)}, f32[3,2,32,256]{3,2,1,0:T(8,128)S(1)}, u32[]{:S(2)}, u32[]{:S(2)}) collective-permute-start(f32[3,2,32,256]{3,2,1,0:T(8,128)S(1)} %get-tuple-element.316), channel_id=1, source_target_pairs={{0,1},{1,2},{2,3},{3,4},{4,5},{5,6},{6,7},{8,9},{9,10},{10,11},{11... | collective-permute-start | bytes 589832 | tf_op jit(solution)/shard_map/ppermute | solution.py:19
  69.5 339.0 %collective-permute-start.14 = (f32[3,2,32,256]{3,2,1,0:T(8,128)S(1)}, f32[3,2,32,256]{3,2,1,0:T(8,128)}, u32[]{:S(2)}, u32[]{:S(2)}) collective-permute-start(f32[3,2,32,256]{3,2,1,0:T(8,128)S(1)} %get-tuple-element.317), channel_id=1, source_target_pairs={{1,0},{2,1},{3,2},{4,3},{5,4},{6,5},{7,6},{9,8},{10,9},{11,10},{12... | collective-permute-start | bytes 589832 | tf_op jit(solution)/shard_map/ppermute | solution.py:20
  96.6 7.5 collective-permute-start
  372.2 29.9 %collective-permute-start.29 = (f32[4,8,64]{2,1,0:T(8,128)S(1)}, f32[4,8,64]{2,1,0:T(8,128)S(1)}, u32[]{:S(2)}, u32[]{:S(2)}) collective-permute-start(f32[4,8,64]{2,1,0:T(8,128)S(1)} %get-tuple-element.230), channel_id=1, source_target_pairs={{0,1},{1,2},{2,3},{3,4},{4,5},{5,6},{6,7},{8,9},{9,10},{10,11},{11... | collective-permute-start | bytes 24584 | tf_op jit(solution)/shard_map/ppermute | solution.py:19
  400.8 7.7 collective-permute-start.12
  402.1 28.4 %collective-permute-start.30 = (f32[4,8,64]{2,1,0:T(8,128)S(1)}, f32[4,8,64]{2,1,0:T(8,128)S(1)}, u32[]{:S(2)}, u32[]{:S(2)}) collective-permute-start(f32[4,8,64]{2,1,0:T(8,128)S(1)} %get-tuple-element.230), channel_id=1, source_target_pairs={{1,0},{2,1},{3,2},{4,3},{5,4},{6,5},{7,6},{9,8},{10,9},{11,10},{12... | collective-permute-start | bytes 24584 | tf_op jit(solution)/shard_map/ppermute | solution.py:20
  414.5 7.7 collective-permute-start.16
  429.2 7.7 collective-permute-start.18
  441.5 7.7 collective-permute-start.20
  453.9 8.0 collective-permute-start.22
  465.5 8.4 collective-permute-start.24
  478.8 7.7 collective-permute-start.26
  491.1 7.7 collective-permute-start.28
  827.3 14.0 %collective-permute-start.33 = (f32[16,32,256]{2,1,0:T(8,128)S(1)}, f32[16,32,256]{2,1,0:T(8,128)S(1)}, u32[]{:S(2)}, u32[]{:S(2)}) collective-permute-start(f32[16,32,256]{2,1,0:T(8,128)S(1)} %add.1628), channel_id=1, source_target_pairs={{0,8},{8,16},{16,24},{24,32},{32,40},{40,48},{48,56},{56,64},{64,7... | collective-permute-start | bytes 1572872 | tf_op jit(solution)/shard_map/ppermute | solution.py:28
  842.8 8.0 collective-permute-start.35
  855.8 7.7 collective-permute-start.37
  868.3 7.7 collective-permute-start.39
  880.6 7.7 collective-permute-start.41
  892.9 7.7 collective-permute-start.43
  904.6 7.7 collective-permute-start.45
  916.9 7.7 collective-permute-start.47
  929.2 7.7 collective-permute-start.49
  (164 other events, 1319.7 us)
where the time goes:
time: 1280 us; the launch traced here: 1260 us
  waiting for transfers between devices  621 us (49%)
  starting transfers between devices  381 us (30%)
  local copies, waits for them, and re-layouts  176 us (14%)
  other arithmetic  80.6 us (6%)
    ppermute x66, waiting for transfers between devices, with_halo(): after = lax.ppermute(initial, axis, down)  360 us
    ppermute x46, waiting for transfers between devices, shifted(): return lax.ppermute(array, axis, pairs)  248 us
    ppermute x66, starting transfers between devices, with_halo(): before = lax.ppermute(last, axis, up)  207 us
    ppermute x46, starting transfers between devices, shifted(): return lax.ppermute(array, axis, pairs)  88.3 us
    ppermute x66, starting transfers between devices, with_halo(): after = lax.ppermute(initial, axis, down)  86.2 us
    reshape x4, local copies, waits for them, and re-layouts, expand(): return wide.reshape((4 * sx, 4 * sy, 4 * sz))  60.7 us
    reshape x3, local copies, waits for them, and re-layouts, restrict(): split = field.reshape((sx // 4, 4, sy // 4, 4, sz // 4, 4))  56 us
    broadcast_in_dim x5, local copies, waits for them, and re-layouts, expand(): jnp.broadcast_to(block[:, None, :, None, :, None], (sx, 4, sy, 4, sz, 4))  40.3 us
  transfers between devices with their start and end apart: 178, of which 169 were waited for; matrix products, arithmetic and copies ran while one was open for 8% of the time, Pallas kernels for 0%

commit v1 on v0

v1 whole, which is shorter than its diff:
```python
import jax
import jax.numpy as jnp
from jax import lax
from jax.experimental import pallas as pl
from jax.experimental.pallas import tpu as pltpu
from jax.sharding import PartitionSpec as P


FINE_STEPS = 2
SWEEPS = 8
C_SWEEPS = 4
WINDOW = 40
NEAR = 16
OWN = 32
GROUPS = WINDOW // 4
VMEM = 48 * 1024 * 1024

f32 = jnp.float32


def lane_of():
    return lax.broadcasted_iota(jnp.int32, (8, 128), 1)


def half_mask():
    return lane_of() < 64


def edge_masks():
    lane = lane_of()
    column = lax.rem(lane, 64)
    row = lax.broadcasted_iota(jnp.int32, (8, 128), 0)
    return row == 0, row == 7, column == 0, column == 63


def swap(tile):
    return pltpu.roll(tile, 64, 1)


def row_up(tile, masks):
    return jnp.where(masks[0], 0.0, pltpu.roll(tile, 1, 0))


def row_down(tile, masks):
    return jnp.where(masks[1], 0.0, pltpu.roll(tile, 7, 0))


def lane_up(tile, masks):
    return jnp.where(masks[2], 0.0, pltpu.roll(tile, 1, 1))


def lane_down(tile, masks):
    return jnp.where(masks[3], 0.0, pltpu.roll(tile, 127, 1))


def sweep(source, target, scaled, weight_ref, first, masks):
    def body(i, carry):
        weight = weight_ref[lax.shift_right_logical(i, 2)]
        cur = [source[i, p] for p in range(16)]
        for p in range(16):
            yi, zi = p // 4, p % 4
            total = source[i - 1, p] + source[i + 1, p]
            above = cur[p - 4] if yi > 0 else row_up(cur[p + 12], masks)
            below = cur[p + 4] if yi < 3 else row_down(cur[p - 12], masks)
            left = cur[p - 1] if zi > 0 else lane_up(cur[p + 3], masks)
            right = cur[p + 1] if zi < 3 else lane_down(cur[p - 3], masks)
            total = total + ((above + below) + (left + right))
            target[i, p] = scaled[i, p] + weight * total
        return carry

    lax.fori_loop(first, WINDOW, body, 0)
    fold(target)


def fold(buffer):
    for p in range(16):
        buffer[WINDOW, p] = swap(buffer[WINDOW - 1, p])


def propagate(even, odd, scaled, inverse_ref, weight_ref, source_ref, first):
    masks = edge_masks()
    for step in range(FINE_STEPS):
        start = first + step * SWEEPS

        def prepare(i, carry):
            k = lax.shift_right_logical(i, 2)
            inverse, source = inverse_ref[k], source_ref[k]
            for p in range(16):
                scaled[i, p] = (even[i, p] + source) * inverse
            return carry

        lax.fori_loop(start, WINDOW, prepare, 0)

        def pair(j, carry):
            sweep(even, odd, scaled, weight_ref, start + 2 * j + 1, masks)
            sweep(odd, even, scaled, weight_ref, start + 2 * j + 2, masks)
            return carry

        lax.fori_loop(0, SWEEPS // 2, pair, 0)


def fill(buffer, tiles_ref, first):
    def body(i, carry):
        tile = tiles_ref[lax.shift_right_logical(i, 2)]
        for p in range(16):
            buffer[i, p] = tile
        return carry

    lax.fori_loop(first, WINDOW, body, 0)
    fold(buffer)


def fill_blocks(buffer, own, left, right):
    half = half_mask()

    def body(j, carry):
        for p in range(16):
            buffer[NEAR + j, p] = jnp.where(half, left[j, p], right[j, p])
            buffer[NEAR + 15 - j, p] = swap(jnp.where(half, right[j, p], left[j, p]))
            buffer[OWN + j, p] = own[j, p]
        return carry

    lax.fori_loop(0, 8, body, 0)
    fold(buffer)


def restrict_own(buffer):
    tiles = []
    for k in range(2):
        total = None
        for i in range(4):
            for p in range(16):
                tile = buffer[OWN + 4 * k + i, p]
                total = tile if total is None else total + tile
        tiles.append(total * (1.0 / 64.0))
    return tiles


def coarse_sweep(field, scaled, weight, masks):
    result = []
    for i in range(16):
        here = field[i]
        beyond = field[i + 1] if i < 15 else swap(here)
        total = (row_up(here, masks) + row_down(here, masks)) + (
            lane_up(here, masks) + lane_down(here, masks)
        )
        total = total + (beyond + field[i - 1] if i > 0 else beyond)
        result.append(scaled[i] + weight[i] * total)
    return result


def blocks_to_global(load, half):
    tiles = []
    for i in range(16):
        block, place = i // 4, i % 4
        if place < 2:
            tiles.append(jnp.where(half, load(block, place), load(7 - block, place)))
        else:
            tiles.append(
                swap(jnp.where(half, load(7 - block, 3 - place), load(block, 3 - place)))
            )
    return tiles


def spread(padded, tiles, half):
    for i in range(16):
        other = swap(tiles[i])
        padded[8 + i] = jnp.where(half, tiles[i], other)
        padded[39 - i] = jnp.where(half, other, tiles[i])


def window_tile(padded, space, k, half):
    return jnp.where(half, padded[4 * space + k], padded[4 * space + 19 - k])


def difference_chain(received, shift, table_ref, ends, masks, half):
    def body(m, delta):
        scaled = [delta[i] * table_ref[0, i] for i in range(16)]
        weight = [table_ref[1, i] for i in range(16)]
        field = list(delta)
        for _ in range(C_SWEEPS):
            field = coarse_sweep(field, scaled, weight, masks)
        for i in range(16):
            ends[m, i] = field[i]
        sender = jnp.minimum(m + shift, 15)
        added = blocks_to_global(lambda b, k: received[sender * 8 + b, k], half)
        return tuple(field[i] + added[i] for i in range(16))

    zero = jnp.zeros((8, 128), f32)
    lax.fori_loop(0, 16, body, (zero,) * 16)


def split_dot(values, matrix):
    high = values.astype(jnp.bfloat16)
    rest = values - high.astype(f32)
    middle = rest.astype(jnp.bfloat16)
    low = (rest - middle.astype(f32)).astype(jnp.bfloat16)

    def dot(part):
        return jnp.dot(part, matrix, preferred_element_type=f32)

    return dot(high) + (dot(middle) + dot(low))


def interleave_matrix(transposed):
    rows = lax.broadcasted_iota(jnp.int32, (256, 256), 0)
    columns = lax.broadcasted_iota(jnp.int32, (256, 256), 1)
    z, c = (columns, rows) if transposed else (rows, columns)
    hit = z == 4 * lax.rem(c, 64) + lax.div(c, 64)
    return jnp.where(hit, 1.0, 0.0).astype(jnp.bfloat16)


def to_phases(initial, labels, block, send, narrow, left, right):
    half = half_mask()
    matrix = interleave_matrix(False)
    for side in range(2):
        lanes = pl.ds(side * 128, 128)
        narrow[side] = initial[:, :, lanes].reshape(512, 128)
        for plane in range(16):
            for yi in range(4):
                rows = pl.ds(plane * 32 + yi, 8, stride=4)
                left[pl.ds(plane * 32 + yi * 8, 8), lanes] = narrow[side, rows, :]
    right[...] = split_dot(left[...], matrix)
    sums = []
    for k in range(2):
        total = jnp.zeros((8, 128), f32)
        for i in range(4 * k, 4 * k + 4):
            for yi in range(4):
                for pair in range(2):
                    lanes = pl.ds(pair * 128, 128)
                    a = right[pl.ds(i * 32 + yi * 8, 8), lanes]
                    b = right[pl.ds((15 - i) * 32 + yi * 8, 8), lanes]
                    even = jnp.where(half, a, swap(b))
                    odd = jnp.where(half, swap(a), b)
                    block[i, yi * 4 + 2 * pair] = even
                    block[i, yi * 4 + 2 * pair + 1] = odd
                    total = total + (even + odd)
        sums.append(total * (1.0 / 64.0))
    tags = [
        jnp.concatenate([labels[k], labels[3 - k]], axis=1).astype(f32) for k in range(2)
    ]
    for peer in range(8):
        for k in range(2):
            send[peer, k] = sums[k]
            send[peer, 2 + k] = tags[k]


def regions(tags, values):
    total = jnp.where(tags == 0.0, values[0], 0.0)
    for region in range(1, len(values)):
        total = jnp.where(tags == region, values[region], total)
    return total


def first_sweeps(
    place, rates, heat, received, block, left, right,
    send, end_block, base, fine, table, window,
    chain, padded, even, odd, scaled, local,
):
    half = half_mask()
    masks = edge_masks()
    index, space = place[0], place[1]
    before = jnp.maximum(index - 1, 0)
    count = 6
    rate_values = [rates[r] for r in range(count)]
    tags = blocks_to_global(lambda b, k: received[b, 2 + k], half)
    start = blocks_to_global(lambda b, k: received[b, k], half)
    for i in range(16):
        rate = FINE_STEPS * regions(tags[i], rate_values) / 16.0
        inverse = 1.0 / (1.0 + 6.0 * rate)
        table[0, i] = inverse
        table[1, i] = rate * inverse
        table[2, i] = tags[i]
        chain[0, i] = start[i]

    outside = jnp.full((8, 128), -1.0, f32)
    for i in range(8):
        padded[i] = outside
        padded[40 + i] = outside
    spread(padded, tags, half)
    for k in range(GROUPS):
        tag = window_tile(padded, space, k, half)
        rate = regions(tag, rate_values)
        inverse = jnp.where(tag < 0.0, 0.0, 1.0 / (1.0 + 6.0 * rate))
        fine[0, k] = inverse
        fine[1, k] = rate * inverse
        fine[2, k] = regions(tag, [heat[before, r] for r in range(count)])
        fine[3, k] = regions(tag, [heat[index, r] for r in range(count)])

    def advance(m, state):
        values = [FINE_STEPS * heat[m, r] for r in range(count)]
        weight = [table[1, i] for i in range(16)]
        rows = [
            (state[i] + regions(table[2, i], values)) * table[0, i] for i in range(16)
        ]
        field = list(state)
        for _ in range(C_SWEEPS):
            field = coarse_sweep(field, rows, weight, masks)
        for i in range(16):
            chain[m + 1, i] = field[i]
        return tuple(field)

    lax.fori_loop(0, 16, advance, tuple(start))

    nothing = jnp.zeros((8, 128), f32)
    for i in range(8):
        padded[i] = nothing
        padded[40 + i] = nothing
    spread(padded, [chain[before + 1, i] for i in range(16)], half)
    before_end = [window_tile(padded, space, 8 + k, half) for k in range(2)]
    spread(padded, [chain[index + 1, i] for i in range(16)], half)
    for k in range(2):
        base[k] = window_tile(padded, space, 8 + k, half)
    spread(padded, [chain[before, i] for i in range(16)], half)
    for k in range(GROUPS):
        window[k] = window_tile(padded, space, k, half)

    for k in range(3):
        local[k] = fine[k]

    @pl.when(index >= 2)
    def _():
        fill(even, window, NEAR)

    @pl.when(index < 2)
    def _():
        fill_blocks(even, block, left, right)

    propagate(even, odd, scaled, local.at[0], local.at[1], local.at[2], NEAR)
    means = restrict_own(even)
    for k in range(2):
        delta = means[k] - before_end[k]

        def put(peer, carry):
            send[peer, k] = delta
            return carry

        lax.fori_loop(0, 128, put, 0)

    @pl.when(index == 0)
    def _():
        end_block[...] = block[...]

    @pl.when(index > 0)
    def _():
        end_block[...] = even[pl.ds(OWN, 8)]


def wide_sweeps(place, fine, window, state, even, odd, scaled):
    @pl.when(place[0] >= 2)
    def _():
        fill(even, window, 0)
        propagate(even, odd, scaled, fine.at[0], fine.at[1], fine.at[2], 0)
        state[...] = even[pl.ds(NEAR, WINDOW - NEAR)]


def second_sweeps(
    place, received, state, end_block, left, right, base, fine, table,
    send, result,
    ends, padded, even, odd, scaled, window,
):
    half = half_mask()
    masks = edge_masks()
    index, space = place[0], place[1]
    before = jnp.maximum(index - 1, 0)
    difference_chain(received, 1, table, ends, masks, half)

    nothing = jnp.zeros((8, 128), f32)
    for i in range(8):
        padded[i] = nothing
        padded[40 + i] = nothing
    spread(padded, [ends[index, i] for i in range(16)], half)
    own_end = [window_tile(padded, space, 8 + k, half) + base[k] for k in range(2)]
    spread(padded, [ends[before, i] for i in range(16)], half)
    keep = jnp.where(index > 0, 1.0, 0.0)
    for k in range(GROUPS):
        window[k] = window_tile(padded, space, k, half) * keep

    @pl.when(index >= 2)
    def _():
        even[pl.ds(NEAR, WINDOW - NEAR)] = state[...]

    @pl.when(index < 2)
    def _():
        fill_blocks(even, end_block, left, right)

    def correct(i, carry):
        tile = window[lax.shift_right_logical(i, 2)]
        for p in range(16):
            even[i, p] = even[i, p] + tile
        return carry

    lax.fori_loop(NEAR, WINDOW, correct, 0)
    fold(even)
    propagate(even, odd, scaled, fine.at[0], fine.at[1], fine.at[3], NEAR)
    result[...] = even[pl.ds(OWN, 8)]
    means = restrict_own(even)
    after = jnp.minimum(index + 1, 15) * 8 + space
    for k in range(2):
        change = (means[k] - own_end[k]) - received[after, k]

        def put(peer, carry):
            send[peer, k] = change
            return carry

        lax.fori_loop(0, 128, put, 0)


def finish(place, received, field, table, out, ends, padded, narrow, left, right):
    half = half_mask()
    masks = edge_masks()
    index, space = place[0], place[1]
    difference_chain(received, 0, table, ends, masks, half)
    spread(padded, [ends[index, i] for i in range(16)], half)
    matrix = interleave_matrix(True)
    for k in range(2):
        tile = window_tile(padded, space, 8 + k, half)
        for i in range(4 * k, 4 * k + 4):
            for yi in range(4):
                for pair in range(2):
                    p = yi * 4 + 2 * pair
                    even, odd = field[i, p] + tile, field[i, p + 1] + tile
                    lanes = pl.ds(pair * 128, 128)
                    left[pl.ds(i * 32 + yi * 8, 8), lanes] = jnp.where(half, even, swap(odd))
                    left[pl.ds((15 - i) * 32 + yi * 8, 8), lanes] = jnp.where(
                        half, swap(even), odd
                    )
    right[...] = split_dot(left[...], matrix)
    for side in range(2):
        lanes = pl.ds(side * 128, 128)
        for plane in range(16):
            for yi in range(4):
                rows = pl.ds(plane * 32 + yi, 8, stride=4)
                narrow[side, rows, :] = right[pl.ds(plane * 32 + yi * 8, 8), lanes]
        out[0, :, :, lanes] = narrow[side].reshape(16, 32, 128)


def call(kernel, operands, results, scratch, scalars=1, flops=0):
    specs = [pl.BlockSpec(memory_space=pltpu.SMEM)] * scalars
    specs += [pl.BlockSpec(memory_space=pltpu.VMEM)] * (len(operands) - scalars)
    shapes = [jax.ShapeDtypeStruct(shape, f32) for shape in results]
    out_specs = [pl.BlockSpec(memory_space=pltpu.VMEM)] * len(results)
    moved = sum(4 * x.size for x in operands) + sum(4 * x.size for x in shapes)
    return pl.pallas_call(
        kernel,
        out_shape=shapes,
        in_specs=specs,
        out_specs=out_specs,
        scratch_shapes=[pltpu.VMEM(shape, f32) for shape in scratch],
        compiler_params=pltpu.CompilerParams(vmem_limit_bytes=VMEM),
        cost_estimate=pl.CostEstimate(flops=flops, bytes_accessed=moved, transcendentals=0),
        name=kernel.__name__,
    )(*operands)


def on_device(initial_temp, region_labels, region_rate, heat_rate):
    peers = lax.axis_size("space")
    index, space = lax.axis_index("tm"), lax.axis_index("space")
    place = jnp.stack([index, space]).astype(jnp.int32)
    tile = (8, 128)
    block_shape = (8, 16) + tile
    wide_shape = (WINDOW + 1, 16) + tile

    block, send = call(
        to_phases, (initial_temp, region_labels),
        (block_shape, (8, 4) + tile), [(2, 512, 128), (512, 256), (512, 256)], scalars=0,
    )

    def beside(array, slices):
        def pairs(by):
            return [
                (t * peers + s, t * peers + s + by)
                for t in slices for s in range(peers) if 0 <= s + by < peers
            ]
        axes = ("tm", "space")
        return lax.ppermute(array, axes, pairs(1)), lax.ppermute(array, axes, pairs(-1))

    left, right = beside(block, (1,))
    received = lax.all_to_all(
        send.reshape(8 * 32, 128), "space", 0, 0, tiled=True
    ).reshape((8, 4) + tile)

    send, end_block, base, fine, table, window = call(
        first_sweeps,
        (place, region_rate, heat_rate, received, block, left, right),
        ((128, 2) + tile, block_shape, (2,) + tile, (4, GROUPS) + tile,
         (3, 16) + tile, (GROUPS,) + tile),
        [(17, 16) + tile, (48,) + tile, wide_shape, wide_shape, wide_shape, (3, GROUPS) + tile],
        scalars=3,
    )

    def gather(array):
        rows = array.reshape(128 * 16, 128)
        rows = lax.all_to_all(rows, ("tm", "space"), 0, 0, tiled=True)
        return rows.reshape((128, 2) + tile)

    received = gather(send)
    left, right = beside(end_block, (0, 1))
    (state,) = call(
        wide_sweeps, (place, fine, window), ((WINDOW - NEAR, 16) + tile,),
        [wide_shape] * 3, flops=10**8,
    )
    send, result = call(
        second_sweeps,
        (place, received, state, end_block, left, right, base, fine, table),
        ((128, 2) + tile, block_shape),
        [(16, 16) + tile, (48,) + tile, wide_shape, wide_shape, wide_shape, (GROUPS,) + tile],
    )
    received = gather(send)
    (out,) = call(
        finish, (place, received, result, table), ((1, 16, 32, 256),),
        [(16, 16) + tile, (48,) + tile, (2, 512, 128), (512, 256), (512, 256)],
    )
    return out


def solution(mesh):
    return jax.shard_map(
        on_device,
        mesh=mesh,
        in_specs=(P("space", None, None), P("space", None, None), P(), P()),
        out_specs=P("tm", "space", None, None),
        check_vma=False,
    )
```

time: 1280 us -> 178 us (0.14); the launches traced: 1260 us -> 176 us
  waiting for transfers between devices: 621 us -> 7.08 us
  starting transfers between devices: 381 us -> 19.7 us
  local copies, waits for them, and re-layouts: 176 us -> 7.99 us
  Pallas kernels: 0 us -> 113 us
  other arithmetic: 80.6 us -> 0.07 us
  blocking collectives: 0 us -> 27.8 us
    ppermute x178 -> x4, waiting for transfers between devices: 621 us -> 0.01 us  [the longest x2 0.01 us: beside(): lax.ppermute(array, axes, pairs(1))]
    ppermute x178 -> x4, starting transfers between devices: 381 us -> 2.76 us  [the longest x2 1.39 us: beside(): lax.ppermute(array, axes, pairs(1))]
    reshape x7 -> x0, local copies, waits for them, and re-layouts: 117 us -> none  [the longest x4 60.7 us: expand(): return wide.reshape((4 * sx, 4 * sy, 4 * sz))]
    pallas_call x0 -> x5, Pallas kernels: none -> 113 us  [call(): pl.pallas_call(kernel, out_shape=shapes, in_specs=specs, out_specs=out_sp...]
    add x272 -> x0, other arithmetic: 41.6 us -> none  [the longest x32 20.4 us: on_device(): fine_field_ext = fine_scaled + fine_coeffs[1] * neighbours(fine_field_ext)]
    broadcast_in_dim x5 -> x0, local copies, waits for them, and re-layouts: 40.3 us -> none  [expand(): jnp.broadcast_to(block[:, None, :, None, :, None], (sx, 4, sy, 4, sz, 4))]
    all_to_all x0 -> x1, blocking collectives: none -> 27.8 us  [gather(): rows = lax.all_to_all(rows, ('tm', 'space'), 0, 0, tiled=True)]
    reduce_sum x3 -> x0, other arithmetic: 21.7 us -> none  [restrict(): return jnp.mean(split, axis=(1, 3, 5))]
  transfers between devices with their start and end apart: 178 -> 6, of which waited for: 169 -> 1; matrix products, arithmetic and copies ran while one was open for 8% -> 0% of each run, Pallas kernels for 0% -> 25%
where the time goes in v1:
time: 178 us; the launch traced here: 176 us
  Pallas kernels  113 us (63%)
  blocking collectives  27.8 us (16%)
  starting transfers between devices  19.7 us (11%)
  local copies, waits for them, and re-layouts  7.99 us (4%)
  waiting for transfers between devices  7.08 us (4%)
    pallas_call x5, Pallas kernels, call(): pl.pallas_call(kernel, out_shape=shapes, in_specs=specs, out_specs=out_sp...  113 us
    all_to_all x1, blocking collectives, gather(): rows = lax.all_to_all(rows, ('tm', 'space'), 0, 0, tiled=True)  27.8 us
    all_to_all x1, starting transfers between devices, gather(): rows = lax.all_to_all(rows, ('tm', 'space'), 0, 0, tiled=True)  10.9 us
    unnamed x21, local copies, waits for them, and re-layouts  7.99 us
    all_to_all x1, waiting for transfers between devices, on_device(): lax.all_to_all(send.reshape(8 * 32, 128), 'space', 0, 0, tiled=True)  7.07 us
    all_to_all x1, starting transfers between devices, on_device(): lax.all_to_all(send.reshape(8 * 32, 128), 'space', 0, 0, tiled=True)  6.05 us
  transfers between devices with their start and end apart: 6, of which 1 were waited for; matrix products, arithmetic and copies ran while one was open for 0% of the time, Pallas kernels for 25%

profile of v1, /device:TPU:8, one launch (start us, length us, event | category | flops | bytes accessed | tf_op | source)
XLA Modules:
  0.0 176.1 jit_solution(1606631281076750746)
XLA Ops:
  0.0 1.0 copy-done.4
  1.0 0.7 copy-done.5
  1.8 1.2 to_phases.1
  3.0 0.7 collective-permute-start.1
  3.6 0.7 collective-permute-start
  4.4 6.0 %all-to-all-start = ((f32[8,32,128]{2,1,0:T(8,128)}), f32[8,32,128]{2,1,0:T(8,128)S(1)}, u32[]{:S(2)}, u32[]{:S(2)}) async-start(f32[8,32,128]{2,1,0:T(8,128)} %bitcast.2), calls=%async_computation | async-start | bytes 262144 | tf_op jit(solution)/shard_map/all_to_all | solution.py:479
  10.4 0.8 copy.5.heat
  11.2 0.1 pad_add_fusion.place
  11.2 7.1 %all-to-all-done = f32[8,32,128]{2,1,0:T(8,128)S(1)} async-done(((f32[8,32,128]{2,1,0:T(8,128)}), f32[8,32,128]{2,1,0:T(8,128)S(1)}, u32[]{:S(2)}, u32[]{:S(2)}) %all-to-all-start) | async-done | bytes 131104 | tf_op jit(solution)/shard_map/all_to_all | solution.py:479
  18.3 0.7 copy-done.9
  19.0 31.1 %first_sweeps.1 = (f32[128,2,8,128]{3,2,1,0:T(8,128)}, f32[8,16,8,128]{3,2,1,0:T(8,128)S(1)}, f32[2,8,128]{2,1,0:T(8,128)S(1)}, f32[4,10,8,128]{3,2,1,0:T(8,128)...) custom-call(s32[2]{0:T(128)S(1)} %pad_add_fusion.place, f32[6]{0:T(128)S(1)} %copy-done.9, ...), custom_call_target="tpu_custom_call" | custom-call | bytes 3686816 | tf_op jit(solution)/shard_map/first_sweeps/pallas_call | solution.py:444
  50.1 10.9 %all-to-all-start.1 = ((f32[128,16,128]{2,1,0:T(8,128)}), f32[128,16,128]{2,1,0:T(8,128)S(1)}, u32[]{:S(2)}, u32[]{:S(2)}) async-start(f32[128,16,128]{2,1,0:T(8,128)} %bitcast.4), calls=%async_computation.1 | async-start | bytes 2097152 | tf_op jit(solution)/shard_map/all_to_all | solution.py:494
  61.0 0.7 collective-permute-start.3
  61.7 0.7 collective-permute-start.2
  62.4 0.6 copy-done.7
  63.0 44.1 %wide_sweeps.1.state = f32[24,16,8,128]{3,2,1,0:T(8,128)S(1)} custom-call(s32[2]{0:T(128)S(1)} %copy-done.7, f32[4,10,8,128]{3,2,1,0:T(8,128)S(1)} %get-tuple-element.18.fine, f32[10,8,128]{2,1,0:T(8,128)S(1)} %get-tuple-element.19.window), custom_call_target="tpu_custom_call" | custom-call | flops 100000000 | bytes 1777672 | tf_op jit(solution)/shard_map/wide_sweeps/pallas_call | solution.py:444
  107.1 0.8 copy-done
  107.9 0.8 copy-done.2
  108.7 1.0 copy-done.1
  109.7 1.0 copy-done.3
  110.8 0.6 copy-done.8
  111.3 29.8 %second_sweeps.1 = (f32[128,2,8,128]{3,2,1,0:T(8,128)S(1)}, f32[8,16,8,128]{3,2,1,0:T(8,128)S(1)}) custom-call(s32[2]{0:T(128)S(1)} %copy-done.8, f32[128,2,8,128]{3,2,1,0:T(8,128)S(1)} %bitcast.8, f32[24,16,8,128]{3,2,1,0:T(8,128)S(1)} %wide_sweeps.1.state, f32[8,16,8,128]{3,2,1,0:T(8,128)S(1)} %get-tuple-element.20.end_block, ...), custom_call_target="tpu_custom_call" | custom-call | bytes 6135816 | tf_op jit(solution)/shard_map/second_sweeps/pallas_call | solution.py:444
  141.1 27.8 %all_to_all.27 = f32[128,16,128]{2,1,0:T(8,128)S(1)} all-to-all(f32[128,16,128]{2,1,0:T(8,128)S(1)} %bitcast.10), channel_id=1, replica_groups=mesh['tm'=16,'space'=8] {'tm','space'}, dimensions={0} | all-to-all | bytes 2097152 | tf_op jit(solution)/shard_map/all_to_all | solution.py:494
  169.0 7.2 %finish.1 = f32[1,16,32,256]{3,2,1,0:T(8,128)} custom-call(s32[2]{0:T(128)S(1)} %copy-done.8, f32[128,2,8,128]{3,2,1,0:T(8,128)S(1)} %bitcast.9, f32[8,16,8,128]{3,2,1,0:T(8,128)S(1)} %get-tuple-element.24.field, f32[3,16,8,128]{3,2,1,0:T(8,128)S(1)} %get-tuple-element.22.table), custom_call_target="tpu_custom_call" | custom-call | bytes 2293768 | tf_op jit(solution)/shard_map/finish/pallas_call | solution.py:444
  (16 shorter events, 0.0 us)
Async XLA Ops:
  0.0 1.0 copy-start.4
  1.0 0.7 copy-start.5
  3.0 15.4 %collective-permute-start.1 = (f32[8,16,8,128]{3,2,1,0:T(8,128)S(1)}, f32[8,16,8,128]{3,2,1,0:T(8,128)S(1)}, u32[]{:S(2)}, u32[]{:S(2)}) collective-permute-start(f32[8,16,8,128]{3,2,1,0:T(8,128)S(1)} %get-tuple-element.16.block), channel_id=1, source_target_pairs={{9,8},{10,9},{11,10},{12,11},{13,12},{14,13},{15,14}} | collective-permute-start | bytes 1572872 | tf_op jit(solution)/shard_map/ppermute | solution.py:476
  3.6 14.7 %collective-permute-start = (f32[8,16,8,128]{3,2,1,0:T(8,128)S(1)}, f32[8,16,8,128]{3,2,1,0:T(8,128)S(1)}, u32[]{:S(2)}, u32[]{:S(2)}) collective-permute-start(f32[8,16,8,128]{3,2,1,0:T(8,128)S(1)} %get-tuple-element.16.block), channel_id=1, source_target_pairs={{8,9},{9,10},{10,11},{11,12},{12,13},{13,14},{14,15}} | collective-permute-start | bytes 1572872 | tf_op jit(solution)/shard_map/ppermute | solution.py:476
  4.4 14.0 %all-to-all-start = ((f32[8,32,128]{2,1,0:T(8,128)}), f32[8,32,128]{2,1,0:T(8,128)S(1)}, u32[]{:S(2)}, u32[]{:S(2)}) async-start(f32[8,32,128]{2,1,0:T(8,128)} %bitcast.2), calls=%async_computation | async-start | bytes 262144 | tf_op jit(solution)/shard_map/all_to_all | solution.py:479
  11.2 38.9 %copy-start.6 = (s32[2]{0:T(128)}, s32[2]{0:T(128)S(1)}, u32[]{:S(2)}) copy-start(s32[2]{0:T(128)S(1)} %pad_add_fusion.place) | copy-start | bytes 28
  18.3 0.7 copy-start.9
  50.1 58.6 %all-to-all-start.1 = ((f32[128,16,128]{2,1,0:T(8,128)}), f32[128,16,128]{2,1,0:T(8,128)S(1)}, u32[]{:S(2)}, u32[]{:S(2)}) async-start(f32[128,16,128]{2,1,0:T(8,128)} %bitcast.4), calls=%async_computation.1 | async-start | bytes 2097152 | tf_op jit(solution)/shard_map/all_to_all | solution.py:494
  61.0 46.1 %collective-permute-start.3 = (f32[8,16,8,128]{3,2,1,0:T(8,128)S(1)}, f32[8,16,8,128]{3,2,1,0:T(8,128)S(1)}, u32[]{:S(2)}, u32[]{:S(2)}) collective-permute-start(f32[8,16,8,128]{3,2,1,0:T(8,128)S(1)} %get-tuple-element.20.end_block), channel_id=1, source_target_pairs={{1,0},{2,1},{3,2},{4,3},{5,4},{6,5},{7,6},{9,8},{10,9},{11,10},{12... | collective-permute-start | bytes 1572872 | tf_op jit(solution)/shard_map/ppermute | solution.py:476
  61.7 46.2 %collective-permute-start.2 = (f32[8,16,8,128]{3,2,1,0:T(8,128)S(1)}, f32[8,16,8,128]{3,2,1,0:T(8,128)S(1)}, u32[]{:S(2)}, u32[]{:S(2)}) collective-permute-start(f32[8,16,8,128]{3,2,1,0:T(8,128)S(1)} %get-tuple-element.20.end_block), channel_id=1, source_target_pairs={{0,1},{1,2},{2,3},{3,4},{4,5},{5,6},{6,7},{8,9},{9,10},{10,11},{11... | collective-permute-start | bytes 1572872 | tf_op jit(solution)/shard_map/ppermute | solution.py:476
  62.4 0.6 copy-start.7
  107.1 0.8 copy-start
  107.9 0.8 copy-start.2
  108.7 1.0 copy-start.1
  109.7 1.0 copy-start.3
  110.8 0.6 copy-start.8

commit v2 on v1

--- a/solution.py
+++ b/solution.py
@@ -13,13 +13,19 @@
 NEAR = 16
 OWN = 32
 GROUPS = WINDOW // 4
-VMEM = 48 * 1024 * 1024
+UNROLL = 8
+VMEM = 24 * 1024 * 1024
+WIDE_VMEM = 62 * 1024 * 1024
 
 f32 = jnp.float32
 
 
 def lane_of():
     return lax.broadcasted_iota(jnp.int32, (8, 128), 1)
+
+
+def coordinates():
+    return lax.axis_index("tm"), lax.axis_index("space")
 
 
 def half_mask():
@@ -53,86 +59,100 @@
     return jnp.where(masks[3], 0.0, pltpu.roll(tile, 127, 1))
 
 
-def sweep(source, target, scaled, weight_ref, first, masks):
-    def body(i, carry):
-        weight = weight_ref[lax.shift_right_logical(i, 2)]
-        cur = [source[i, p] for p in range(16)]
-        for p in range(16):
-            yi, zi = p // 4, p % 4
-            total = source[i - 1, p] + source[i + 1, p]
-            above = cur[p - 4] if yi > 0 else row_up(cur[p + 12], masks)
-            below = cur[p + 4] if yi < 3 else row_down(cur[p - 12], masks)
-            left = cur[p - 1] if zi > 0 else lane_up(cur[p + 3], masks)
-            right = cur[p + 1] if zi < 3 else lane_down(cur[p - 3], masks)
-            total = total + ((above + below) + (left + right))
-            target[i, p] = scaled[i, p] + weight * total
+def sweep(source, target, scaled, weight_ref, start, stop, masks, fresh=None):
+    def body(t, carry):
+        base = start + UNROLL * t
+        for u in range(UNROLL):
+            i = base + u + 1
+            k = lax.shift_right_logical(base + u, 2)
+            weight = weight_ref[k]
+            if fresh is not None:
+                inverse, heat = fresh[0][k], fresh[1][k]
+            cur = [source[i, p] for p in range(16)]
+            for p in range(16):
+                yi, zi = p // 4, p % 4
+                total = source[i - 1, p] + source[i + 1, p]
+                above = cur[p - 4] if yi > 0 else row_up(cur[p + 12], masks)
+                below = cur[p + 4] if yi < 3 else row_down(cur[p - 12], masks)
+                left = cur[p - 1] if zi > 0 else lane_up(cur[p + 3], masks)
+                right = cur[p + 1] if zi < 3 else lane_down(cur[p - 3], masks)
+                total = total + ((above + below) + (left + right))
+                if fresh is None:
+                    term = scaled[i, p]
+                else:
+                    term = (cur[p] + heat) * inverse
+                    scaled[i, p] = term
+                target[i, p] = term + weight * total
         return carry
 
-    lax.fori_loop(first, WINDOW, body, 0)
-    fold(target)
+    lax.fori_loop(0, stop, body, 0)
 
 
 def fold(buffer):
     for p in range(16):
-        buffer[WINDOW, p] = swap(buffer[WINDOW - 1, p])
-
-
-def propagate(even, odd, scaled, inverse_ref, weight_ref, source_ref, first):
+        buffer[WINDOW + 1, p] = swap(buffer[WINDOW, p])
+
+
+def run_sweeps(even, odd, scaled, inverse_ref, weight_ref, source_ref, first):
     masks = edge_masks()
+
+    def one(source, target, q, fresh=None):
+        group = lax.div(first + q, UNROLL)
+        steps = WINDOW // UNROLL - group
+        sweep(source, target, scaled, weight_ref, UNROLL * group, steps, masks, fresh)
+        fold(target)
+
+    fold(even)
     for step in range(FINE_STEPS):
-        start = first + step * SWEEPS
-
-        def prepare(i, carry):
-            k = lax.shift_right_logical(i, 2)
-            inverse, source = inverse_ref[k], source_ref[k]
+        base = step * SWEEPS
+        one(even, odd, jnp.int32(base + 1), (inverse_ref, source_ref))
+
+        def pair(j, carry):
+            one(odd, even, base + 2 * j + 2)
+            one(even, odd, base + 2 * j + 3)
+            return carry
+
+        lax.fori_loop(0, SWEEPS // 2 - 1, pair, 0)
+        one(odd, even, jnp.int32(base + SWEEPS))
+
+
+def fill(buffer, tiles_ref, first, last):
+    def body(k, carry):
+        tile = tiles_ref[k]
+        for u in range(4):
             for p in range(16):
-                scaled[i, p] = (even[i, p] + source) * inverse
-            return carry
-
-        lax.fori_loop(start, WINDOW, prepare, 0)
-
-        def pair(j, carry):
-            sweep(even, odd, scaled, weight_ref, start + 2 * j + 1, masks)
-            sweep(odd, even, scaled, weight_ref, start + 2 * j + 2, masks)
-            return carry
-
-        lax.fori_loop(0, SWEEPS // 2, pair, 0)
-
-
-def fill(buffer, tiles_ref, first):
-    def body(i, carry):
-        tile = tiles_ref[lax.shift_right_logical(i, 2)]
-        for p in range(16):
-            buffer[i, p] = tile
+                buffer[4 * k + u + 1, p] = tile
         return carry
 
-    lax.fori_loop(first, WINDOW, body, 0)
-    fold(buffer)
-
-
-def fill_blocks(buffer, own, left, right):
+    lax.fori_loop(first, last, body, 0)
+
+
+def fill_sides(buffer, first, left, right):
     half = half_mask()
 
     def body(j, carry):
         for p in range(16):
-            buffer[NEAR + j, p] = jnp.where(half, left[j, p], right[j, p])
-            buffer[NEAR + 15 - j, p] = swap(jnp.where(half, right[j, p], left[j, p]))
-            buffer[OWN + j, p] = own[j, p]
+            buffer[first + j + 1, p] = jnp.where(half, left[j, p], right[j, p])
+            buffer[first + 16 - j, p] = swap(jnp.where(half, right[j, p], left[j, p]))
         return carry
 
     lax.fori_loop(0, 8, body, 0)
-    fold(buffer)
 
 
 def restrict_own(buffer):
     tiles = []
     for k in range(2):
-        total = None
+        parts = []
         for i in range(4):
             for p in range(16):
-                tile = buffer[OWN + 4 * k + i, p]
-                total = tile if total is None else total + tile
-        tiles.append(total * (1.0 / 64.0))
+                tile = buffer[OWN + 4 * k + i + 1, p]
+                if len(parts) < 8:
+                    parts.append(tile)
+                else:
+                    parts[p % 8] = parts[p % 8] + tile
+        while len(parts) > 1:
+            parts = [parts[j] + parts[j + 1] for j in range(0, len(parts), 2)]
+        tiles.append(parts[0] * (1.0 / 64.0))
     return tiles
 
 
@@ -252,14 +272,10 @@
     return total
 
 
-def first_sweeps(
-    place, rates, heat, received, block, left, right,
-    send, end_block, base, fine, table, window,
-    chain, padded, even, odd, scaled, local,
-):
+def first_chain(rates, heat, received, base, fine, table, window, chain, padded):
     half = half_mask()
     masks = edge_masks()
-    index, space = place[0], place[1]
+    index, space = coordinates()
     before = jnp.maximum(index - 1, 0)
     count = 6
     rate_values = [rates[r] for r in range(count)]
@@ -307,61 +323,93 @@
         padded[i] = nothing
         padded[40 + i] = nothing
     spread(padded, [chain[before + 1, i] for i in range(16)], half)
-    before_end = [window_tile(padded, space, 8 + k, half) for k in range(2)]
+    for k in range(2):
+        base[k] = window_tile(padded, space, 8 + k, half)
     spread(padded, [chain[index + 1, i] for i in range(16)], half)
     for k in range(2):
-        base[k] = window_tile(padded, space, 8 + k, half)
+        base[2 + k] = window_tile(padded, space, 8 + k, half)
     spread(padded, [chain[before, i] for i in range(16)], half)
     for k in range(GROUPS):
         window[k] = window_tile(padded, space, k, half)
 
-    for k in range(3):
-        local[k] = fine[k]
+
+def move(pairs, semaphores):
+    copies = [
+        pltpu.make_async_copy(source, target, semaphores.at[j])
+        for j, (source, target) in enumerate(pairs)
+    ]
+    for copy in copies:
+        copy.start()
+    return copies
+
+
+def move_now(pairs, semaphores):
+    for copy in move(pairs, semaphores):
+        copy.wait()
+
+
+def first_sweeps(
+    block, left, right, far_left, far_right, base, fine, window,
+    send, even, odd, scaled, sides, semaphores,
+):
+    index, _ = coordinates()
 
     @pl.when(index >= 2)
     def _():
-        fill(even, window, NEAR)
+        fill(even, window, NEAR // 4, GROUPS)
 
     @pl.when(index < 2)
     def _():
-        fill_blocks(even, block, left, right)
-
-    propagate(even, odd, scaled, local.at[0], local.at[1], local.at[2], NEAR)
+        move_now(
+            [(left, sides.at[0]), (right, sides.at[1]), (block, even.at[pl.ds(OWN + 1, 8)])],
+            semaphores,
+        )
+        fill_sides(even, NEAR, sides.at[0], sides.at[1])
+
+    run_sweeps(even, odd, scaled, fine.at[0], fine.at[1], fine.at[2], NEAR)
     means = restrict_own(even)
     for k in range(2):
-        delta = means[k] - before_end[k]
-
-        def put(peer, carry):
+        delta = means[k] - base[k]
+        for peer in range(128):
             send[peer, k] = delta
-            return carry
-
-        lax.fori_loop(0, 128, put, 0)
-
-    @pl.when(index == 0)
+
+
+def wide_sweeps(
+    fine, window, block, left, right, far_left, far_right,
+    state, even, odd, scaled, sides, semaphores,
+):
+    index, _ = coordinates()
+
+    @pl.when(index < 2)
     def _():
-        end_block[...] = block[...]
+        move_now(
+            [(left, sides.at[0]), (right, sides.at[1]), (far_left, sides.at[2]),
+             (far_right, sides.at[3]), (block, even.at[pl.ds(OWN + 1, 8)])],
+            semaphores,
+        )
+        fill_sides(even, NEAR, sides.at[0], sides.at[1])
+        fill_sides(even, 0, sides.at[2], sides.at[3])
+
+    @pl.when(index >= 2)
+    def _():
+        fill(even, window, 0, GROUPS)
 
     @pl.when(index > 0)
     def _():
-        end_block[...] = even[pl.ds(OWN, 8)]
-
-
-def wide_sweeps(place, fine, window, state, even, odd, scaled):
-    @pl.when(place[0] >= 2)
-    def _():
-        fill(even, window, 0)
-        propagate(even, odd, scaled, fine.at[0], fine.at[1], fine.at[2], 0)
-        state[...] = even[pl.ds(NEAR, WINDOW - NEAR)]
+        run_sweeps(even, odd, scaled, fine.at[0], fine.at[1], fine.at[2], 0)
+
+    move_now([(even.at[pl.ds(NEAR + 1, WINDOW - NEAR)], state)], semaphores.at[pl.ds(0, 1)])
 
 
 def second_sweeps(
-    place, received, state, end_block, left, right, base, fine, table,
+    received, state, base, fine, table,
     send, result,
-    ends, padded, even, odd, scaled, window,
+    ends, padded, even, odd, scaled, window, semaphores,
 ):
     half = half_mask()
     masks = edge_masks()
-    index, space = place[0], place[1]
+    index, space = coordinates()
+    (arrival,) = move([(state, even.at[pl.ds(NEAR + 1, WINDOW - NEAR)])], semaphores)
     before = jnp.maximum(index - 1, 0)
     difference_chain(received, 1, table, ends, masks, half)
 
@@ -370,49 +418,42 @@
         padded[i] = nothing
         padded[40 + i] = nothing
     spread(padded, [ends[index, i] for i in range(16)], half)
-    own_end = [window_tile(padded, space, 8 + k, half) + base[k] for k in range(2)]
+    own_end = [window_tile(padded, space, 8 + k, half) + base[2 + k] for k in range(2)]
     spread(padded, [ends[before, i] for i in range(16)], half)
     keep = jnp.where(index > 0, 1.0, 0.0)
     for k in range(GROUPS):
         window[k] = window_tile(padded, space, k, half) * keep
 
-    @pl.when(index >= 2)
-    def _():
-        even[pl.ds(NEAR, WINDOW - NEAR)] = state[...]
-
-    @pl.when(index < 2)
-    def _():
-        fill_blocks(even, end_block, left, right)
-
-    def correct(i, carry):
-        tile = window[lax.shift_right_logical(i, 2)]
-        for p in range(16):
-            even[i, p] = even[i, p] + tile
+    arrival.wait()
+
+    def correct(k, carry):
+        tile = window[k]
+        for u in range(4):
+            for p in range(16):
+                even[4 * k + u + 1, p] = even[4 * k + u + 1, p] + tile
         return carry
 
-    lax.fori_loop(NEAR, WINDOW, correct, 0)
-    fold(even)
-    propagate(even, odd, scaled, fine.at[0], fine.at[1], fine.at[3], NEAR)
-    result[...] = even[pl.ds(OWN, 8)]
+    lax.fori_loop(NEAR // 4, GROUPS, correct, 0)
+    run_sweeps(even, odd, scaled, fine.at[0], fine.at[1], fine.at[3], NEAR)
+    (copy,) = move([(even.at[pl.ds(OWN + 1, 8)], result)], semaphores)
     means = restrict_own(even)
     after = jnp.minimum(index + 1, 15) * 8 + space
-    for k in range(2):
-        change = (means[k] - own_end[k]) - received[after, k]
-
-        def put(peer, carry):
-            send[peer, k] = change
-            return carry
-
-        lax.fori_loop(0, 128, put, 0)
-
-
-def finish(place, received, field, table, out, ends, padded, narrow, left, right):
+    changes = [(means[k] - own_end[k]) - received[after, k] for k in range(2)]
+    for peer in range(128):
+        for k in range(2):
+            send[peer, k] = changes[k]
+    copy.wait()
+
+
+def finish(received, result, table, out, ends, padded, narrow, left, right, field, semaphores):
     half = half_mask()
     masks = edge_masks()
-    index, space = place[0], place[1]
+    index, space = coordinates()
+    (copy,) = move([(result, field)], semaphores)
     difference_chain(received, 0, table, ends, masks, half)
     spread(padded, [ends[index, i] for i in range(16)], half)
     matrix = interleave_matrix(True)
+    copy.wait()
     for k in range(2):
         tile = window_tile(padded, space, 8 + k, half)
         for i in range(4 * k, 4 * k + 4):
@@ -435,81 +476,96 @@
         out[0, :, :, lanes] = narrow[side].reshape(16, 32, 128)
 
 
-def call(kernel, operands, results, scratch, scalars=1, flops=0):
-    specs = [pl.BlockSpec(memory_space=pltpu.SMEM)] * scalars
-    specs += [pl.BlockSpec(memory_space=pltpu.VMEM)] * (len(operands) - scalars)
-    shapes = [jax.ShapeDtypeStruct(shape, f32) for shape in results]
-    out_specs = [pl.BlockSpec(memory_space=pltpu.VMEM)] * len(results)
-    moved = sum(4 * x.size for x in operands) + sum(4 * x.size for x in shapes)
+def call(kernel, operands, results, scratch, copies=0, flops=0, vmem=VMEM):
+    where = {
+        "scalar": pltpu.SMEM, "near": pltpu.VMEM, "far": pltpu.HBM,
+    }
+    shapes = [jax.ShapeDtypeStruct(shape, f32) for shape, _ in results]
+    arrays = [x for x, _ in operands]
+    moved = sum(4 * x.size for x in arrays) + sum(4 * x.size for x in shapes)
+    semaphores = [pltpu.SemaphoreType.DMA((copies,))] if copies else []
     return pl.pallas_call(
         kernel,
         out_shape=shapes,
-        in_specs=specs,
-        out_specs=out_specs,
-        scratch_shapes=[pltpu.VMEM(shape, f32) for shape in scratch],
-        compiler_params=pltpu.CompilerParams(vmem_limit_bytes=VMEM),
+        in_specs=[pl.BlockSpec(memory_space=where[w]) for _, w in operands],
+        out_specs=[pl.BlockSpec(memory_space=where[w]) for _, w in results],
+        scratch_shapes=[pltpu.VMEM(shape, f32) for shape in scratch] + semaphores,
+        compiler_params=pltpu.CompilerParams(vmem_limit_bytes=vmem),
         cost_estimate=pl.CostEstimate(flops=flops, bytes_accessed=moved, transcendentals=0),
         name=kernel.__name__,
-    )(*operands)
+    )(*arrays)
 
 
 def on_device(initial_temp, region_labels, region_rate, heat_rate):
     peers = lax.axis_size("space")
-    index, space = lax.axis_index("tm"), lax.axis_index("space")
-    place = jnp.stack([index, space]).astype(jnp.int32)
     tile = (8, 128)
     block_shape = (8, 16) + tile
-    wide_shape = (WINDOW + 1, 16) + tile
+    buffer = (WINDOW + 2, 16) + tile
 
     block, send = call(
-        to_phases, (initial_temp, region_labels),
-        (block_shape, (8, 4) + tile), [(2, 512, 128), (512, 256), (512, 256)], scalars=0,
-    )
-
-    def beside(array, slices):
-        def pairs(by):
-            return [
-                (t * peers + s, t * peers + s + by)
-                for t in slices for s in range(peers) if 0 <= s + by < peers
-            ]
-        axes = ("tm", "space")
-        return lax.ppermute(array, axes, pairs(1)), lax.ppermute(array, axes, pairs(-1))
-
-    left, right = beside(block, (1,))
+        to_phases,
+        [(initial_temp, "near"), (region_labels, "near")],
+        [(block_shape, "near"), ((8, 4) + tile, "near")],
+        [(2, 512, 128), (512, 256), (512, 256)],
+    )
+
+    def beside(by, routes):
+        pairs = [
+            (t * peers + s + by, to * peers + s)
+            for t, to in routes for s in range(peers) if 0 <= s + by < peers
+        ]
+        return lax.ppermute(block, ("tm", "space"), pairs)
+
+    sides = [
+        (beside(-1, ((8, 1), (10, 0))), "far"), (beside(1, ((9, 1), (11, 0))), "far"),
+        (beside(-2, ((2, 1),)), "far"), (beside(2, ((6, 1),)), "far"),
+    ]
     received = lax.all_to_all(
         send.reshape(8 * 32, 128), "space", 0, 0, tiled=True
     ).reshape((8, 4) + tile)
 
-    send, end_block, base, fine, table, window = call(
+    base, fine, table, window = call(
+        first_chain,
+        [(region_rate, "scalar"), (heat_rate, "scalar"), (received, "near")],
+        [((4,) + tile, "near"), ((4, GROUPS) + tile, "near"), ((3, 16) + tile, "near"),
+         ((GROUPS,) + tile, "near")],
+        [(17, 16) + tile, (48,) + tile],
+    )
+    base, fine, table, window = ((x, "near") for x in (base, fine, table, window))
+    (send,) = call(
         first_sweeps,
-        (place, region_rate, heat_rate, received, block, left, right),
-        ((128, 2) + tile, block_shape, (2,) + tile, (4, GROUPS) + tile,
-         (3, 16) + tile, (GROUPS,) + tile),
-        [(17, 16) + tile, (48,) + tile, wide_shape, wide_shape, wide_shape, (3, GROUPS) + tile],
-        scalars=3,
+        [(block, "far"), *sides, base, fine, window],
+        [((128, 2) + tile, "near")],
+        [buffer, buffer, buffer, (2,) + block_shape],
+        copies=3,
     )
 
     def gather(array):
         rows = array.reshape(128 * 16, 128)
         rows = lax.all_to_all(rows, ("tm", "space"), 0, 0, tiled=True)
-        return rows.reshape((128, 2) + tile)
+        return (rows.reshape((128, 2) + tile), "near")
 
     received = gather(send)
-    left, right = beside(end_block, (0, 1))
     (state,) = call(
-        wide_sweeps, (place, fine, window), ((WINDOW - NEAR, 16) + tile,),
-        [wide_shape] * 3, flops=10**8,
+        wide_sweeps,
+        [fine, window, (block, "far"), *sides],
+        [((WINDOW - NEAR, 16) + tile, "far")],
+        [buffer, buffer, buffer, (4,) + block_shape],
+        copies=5, flops=10**8, vmem=WIDE_VMEM,
     )
     send, result = call(
         second_sweeps,
-        (place, received, state, end_block, left, right, base, fine, table),
-        ((128, 2) + tile, block_shape),
-        [(16, 16) + tile, (48,) + tile, wide_shape, wide_shape, wide_shape, (GROUPS,) + tile],
-    )
-    received = gather(send)
+        [received, (state, "far"), base, fine, table],
+        [((128, 2) + tile, "near"), (block_shape, "far")],
+        [(16, 16) + tile, (48,) + tile, buffer, buffer, buffer, (GROUPS,) + tile],
+        copies=1,
+    )
     (out,) = call(
-        finish, (place, received, result, table), ((1, 16, 32, 256),),
-        [(16, 16) + tile, (48,) + tile, (2, 512, 128), (512, 256), (512, 256)],
+        finish,
+        [gather(send), (result, "far"), table],
+        [((1, 16, 32, 256), "near")],
+        [(16, 16) + tile, (48,) + tile, (2, 512, 128), (512, 256), (512, 256), block_shape],
+        copies=1,
     )
     return out
 

time: 178 us -> 110 us (0.62)
  Pallas kernels: 113 us -> 51.7 us
  local copies, waits for them, and re-layouts: 7.99 us -> 4.62 us
  waiting for transfers between devices: 7.08 us -> 10.1 us
  blocking collectives: 27.8 us -> 24.9 us
  starting transfers between devices: 19.7 us -> 17.2 us
    pallas_call x5 -> x6, Pallas kernels: 113 us -> 51.7 us  [call(): pl.pallas_call(kernel, out_shape=shapes, in_specs=[pl.BlockSpec(memory_sp...]
    all_to_all x1, starting transfers between devices: 10.9 us -> 5.68 us  [gather(): rows = lax.all_to_all(rows, ('tm', 'space'), 0, 0, tiled=True)]
    ppermute x4, starting transfers between devices: 2.76 us -> 6.22 us  [beside(): return lax.ppermute(block, ('tm', 'space'), pairs)]
    unnamed x21 -> x25, local copies, waits for them, and re-layouts: 7.99 us -> 4.62 us
    all_to_all x1, waiting for transfers between devices: 0.01 us -> 2.93 us  [gather(): rows = lax.all_to_all(rows, ('tm', 'space'), 0, 0, tiled=True)]
    all_to_all x1, blocking collectives: 27.8 us -> 24.9 us  [gather(): rows = lax.all_to_all(rows, ('tm', 'space'), 0, 0, tiled=True)]
  transfers between devices with their start and end apart: 6 -> 6, of which waited for: 1 -> 2; matrix products, arithmetic and copies ran while one was open for 0% -> 1% of each run, Pallas kernels for 25% -> 20%
where the time goes in v2:
time: 110 us; the launch traced here: 109 us
  Pallas kernels  51.7 us (47%)
  blocking collectives  24.9 us (23%)
  starting transfers between devices  17.2 us (16%)
  waiting for transfers between devices  10.1 us (9%)
  local copies, waits for them, and re-layouts  4.62 us (4%)
    pallas_call x6, Pallas kernels, call(): pl.pallas_call(kernel, out_shape=shapes, in_specs=[pl.BlockSpec(memory_sp...  51.7 us
    all_to_all x1, blocking collectives, gather(): rows = lax.all_to_all(rows, ('tm', 'space'), 0, 0, tiled=True)  24.9 us
    all_to_all x1, waiting for transfers between devices, on_device(): lax.all_to_all(send.reshape(8 * 32, 128), 'space', 0, 0, tiled=True)  7.15 us
    ppermute x4, starting transfers between devices, beside(): return lax.ppermute(block, ('tm', 'space'), pairs)  6.22 us
    all_to_all x1, starting transfers between devices, gather(): rows = lax.all_to_all(rows, ('tm', 'space'), 0, 0, tiled=True)  5.68 us
    all_to_all x1, starting transfers between devices, on_device(): lax.all_to_all(send.reshape(8 * 32, 128), 'space', 0, 0, tiled=True)  5.32 us
    unnamed x25, local copies, waits for them, and re-layouts  4.62 us
    all_to_all x1, waiting for transfers between devices, gather(): rows = lax.all_to_all(rows, ('tm', 'space'), 0, 0, tiled=True)  2.93 us
  transfers between devices with their start and end apart: 6, of which 2 were waited for; matrix products, arithmetic and copies ran while one was open for 1% of the time, Pallas kernels for 20%

profile of v2, /device:TPU:8, one launch (start us, length us, event | category | flops | bytes accessed | tf_op | source)
XLA Modules:
  0.0 108.8 jit_solution(4580695332961191632)
XLA Ops:
  0.0 1.0 copy-done.8
  1.0 0.7 copy-done.10
  1.8 1.2 %to_phases.1 = (f32[8,16,8,128]{3,2,1,0:T(8,128)S(1)}, f32[8,4,8,128]{3,2,1,0:T(8,128)}) custom-call(f32[16,32,256]{2,1,0:T(8,128)S(1)} %copy-done.8, s32[4,8,64]{2,1,0:T(8,128)S(1)} %copy-done.10), custom_call_target="tpu_custom_call" | custom-call | bytes 1187840 | tf_op jit(solution)/shard_map/to_phases/pallas_call | solution.py:487
  3.0 0.7 collective-permute-start.3
  3.6 0.7 collective-permute-start.2
  4.3 0.7 collective-permute-start.1
  5.1 4.1 %collective-permute-start = (f32[8,16,8,128]{3,2,1,0:T(8,128)S(1)}, f32[8,16,8,128]{3,2,1,0:T(8,128)S(1)}, u32[]{:S(2)}, u32[]{:S(2)}) collective-permute-start(f32[8,16,8,128]{3,2,1,0:T(8,128)S(1)} %get-tuple-element.13.block), channel_id=1, source_target_pairs={{64,9},{65,10},{66,11},{67,12},{68,13},{69,14},{70,15},{80,1},{81,... | collective-permute-start | bytes 1572872 | tf_op jit(solution)/shard_map/ppermute | solution.py:517
  9.2 5.3 %all-to-all-start = ((f32[8,32,128]{2,1,0:T(8,128)}), f32[8,32,128]{2,1,0:T(8,128)S(1)}, u32[]{:S(2)}, u32[]{:S(2)}) async-start(f32[8,32,128]{2,1,0:T(8,128)} %bitcast), calls=%async_computation | async-start | bytes 262144 | tf_op jit(solution)/shard_map/all_to_all | solution.py:523
  14.5 0.8 copy.5.heat
  15.3 7.1 %all-to-all-done = f32[8,32,128]{2,1,0:T(8,128)S(1)} async-done(((f32[8,32,128]{2,1,0:T(8,128)}), f32[8,32,128]{2,1,0:T(8,128)S(1)}, u32[]{:S(2)}, u32[]{:S(2)}) %all-to-all-start) | async-done | bytes 131104 | tf_op jit(solution)/shard_map/all_to_all | solution.py:523
  22.4 0.7 copy-done.11
  23.1 6.3 %first_chain.1 = (f32[4,8,128]{2,1,0:T(8,128)S(1)}, f32[4,10,8,128]{3,2,1,0:T(8,128)S(1)}, f32[3,16,8,128]{3,2,1,0:T(8,128)S(1)}, f32[10,8,128]{2,1,0:T(8,128)S(1)}) custom-call(f32[6]{0:T(128)S(1)} %copy-done.11, f32[16,6]{1,0:T(8,128)S(1)} %copy.5.heat, f32[8,4,8,128]{3,2,1,0:T(8,128)S(1)} %bitcast.9), custom_call_target="tpu_custom_call" | custom-call | bytes 549272 | tf_op jit(solution)/shard_map/first_chain/pallas_call | solution.py:487
  29.4 0.0 collective-permute-done.3.far_right
  29.4 0.0 collective-permute-done.2.far_left
  29.4 0.0 collective-permute-done.1.right
  29.5 0.0 collective-permute-done.left
  29.5 8.8 %first_sweeps.1 = f32[128,2,8,128]{3,2,1,0:T(8,128)} custom-call(f32[8,16,8,128]{3,2,1,0:T(8,128)S(1)} %get-tuple-element.13.block, f32[8,16,8,128]{3,2,1,0:T(8,128)S(1)} %collective-permute-done.left, f32[8,16,8,128]{3,2,1,0:T(8,128)S(1)} %collective-permute-done.1.right, f32[8,16,8,128]{3,2,1,0:T(8,128)S(1)} %collective-permute-done.2.far_left, ...), custom_call_target="tpu_custom_call" | custom-call | bytes 3891200 | tf_op jit(solution)/shard_map/first_sweeps/pallas_call | solution.py:487
  38.4 5.7 %all-to-all-start.1 = ((f32[128,16,128]{2,1,0:T(8,128)}), f32[128,16,128]{2,1,0:T(8,128)S(1)}, u32[]{:S(2)}, u32[]{:S(2)}) async-start(f32[128,16,128]{2,1,0:T(8,128)} %bitcast.2), calls=%async_computation.1 | async-start | bytes 2097152 | tf_op jit(solution)/shard_map/all_to_all | solution.py:545
  44.1 15.3 %wide_sweeps.1.state = f32[24,16,8,128]{3,2,1,0:T(8,128)} custom-call(f32[4,10,8,128]{3,2,1,0:T(8,128)} %copy-done.6, f32[10,8,128]{2,1,0:T(8,128)} %copy-done.9, f32[8,16,8,128]{3,2,1,0:T(8,128)} %copy-done.1, f32[8,16,8,128]{3,2,1,0:T(8,128)} %copy-done.5, f32[8,16,8,128]{3,2,1,0:T(8,128)} %copy-done.4, f32[8,16,8,128]{3,2,1,0:T(8,128)} %copy-done.3, ...), custom_call_target="tpu_custom_call" | custom-call | flops 100000000 | bytes 4399104 | tf_op jit(solution)/shard_map/wide_sweeps/pallas_call | solution.py:487
  59.4 2.9 %all-to-all-done.1 = f32[128,16,128]{2,1,0:T(8,128)S(1)} async-done(((f32[128,16,128]{2,1,0:T(8,128)}), f32[128,16,128]{2,1,0:T(8,128)S(1)}, u32[]{:S(2)}, u32[]{:S(2)}) %all-to-all-start.1) | async-done | bytes 1048608 | tf_op jit(solution)/shard_map/all_to_all | solution.py:545
  62.3 1.4 %copy-done = f32[24,16,8,128]{3,2,1,0:T(8,128)S(1)} copy-done((f32[24,16,8,128]{3,2,1,0:T(8,128)S(1)}, f32[24,16,8,128]{3,2,1,0:T(8,128)}, u32[]{:S(2)}) %copy-start) | copy-done | bytes 1572888
  63.8 13.4 %second_sweeps.1 = (f32[128,2,8,128]{3,2,1,0:T(8,128)S(1)}, f32[8,16,8,128]{3,2,1,0:T(8,128)S(1)}) custom-call(f32[128,2,8,128]{3,2,1,0:T(8,128)S(1)} %bitcast.6, f32[24,16,8,128]{3,2,1,0:T(8,128)S(1)} %copy-done, f32[4,8,128]{2,1,0:T(8,128)S(1)} %get-tuple-element.15.base, f32[4,10,8,128]{3,2,1,0:T(8,128)S(1)} %copy-done.7, ...), custom_call_target="tpu_custom_call" | custom-call | bytes 4571136 | tf_op jit(solution)/shard_map/second_sweeps/pallas_call | solution.py:487
  77.2 24.9 %all_to_all.27 = f32[128,16,128]{2,1,0:T(8,128)S(1)} all-to-all(f32[128,16,128]{2,1,0:T(8,128)S(1)} %bitcast.8), channel_id=1, replica_groups=mesh['tm'=16,'space'=8] {'tm','space'}, dimensions={0} | all-to-all | bytes 2097152 | tf_op jit(solution)/shard_map/all_to_all | solution.py:545
  102.1 6.7 %finish.1 = f32[1,16,32,256]{3,2,1,0:T(8,128)} custom-call(f32[128,2,8,128]{3,2,1,0:T(8,128)S(1)} %bitcast.7, f32[8,16,8,128]{3,2,1,0:T(8,128)S(1)} %get-tuple-element.20.result, f32[3,16,8,128]{3,2,1,0:T(8,128)S(1)} %get-tuple-element.18.table), custom_call_target="tpu_custom_call" | custom-call | bytes 2293760 | tf_op jit(solution)/shard_map/finish/pallas_call | solution.py:487
  (20 shorter events, 0.0 us)
Async XLA Ops:
  0.0 1.0 copy-start.8
  1.0 0.7 copy-start.10
  3.0 35.4 %copy-start.1 = (f32[8,16,8,128]{3,2,1,0:T(8,128)}, f32[8,16,8,128]{3,2,1,0:T(8,128)S(1)}, u32[]{:S(2)}) copy-start(f32[8,16,8,128]{3,2,1,0:T(8,128)S(1)} %get-tuple-element.13.block) | copy-start | bytes 1572868
  3.0 26.4 %collective-permute-start.3 = (f32[8,16,8,128]{3,2,1,0:T(8,128)S(1)}, f32[8,16,8,128]{3,2,1,0:T(8,128)S(1)}, u32[]{:S(2)}, u32[]{:S(2)}) collective-permute-start(f32[8,16,8,128]{3,2,1,0:T(8,128)S(1)} %get-tuple-element.13.block), channel_id=1, source_target_pairs={{50,8},{51,9},{52,10},{53,11},{54,12},{55,13}} | collective-permute-start | bytes 1572872 | tf_op jit(solution)/shard_map/ppermute | solution.py:517
  3.6 25.8 %collective-permute-start.2 = (f32[8,16,8,128]{3,2,1,0:T(8,128)S(1)}, f32[8,16,8,128]{3,2,1,0:T(8,128)S(1)}, u32[]{:S(2)}, u32[]{:S(2)}) collective-permute-start(f32[8,16,8,128]{3,2,1,0:T(8,128)S(1)} %get-tuple-element.13.block), channel_id=1, source_target_pairs={{16,10},{17,11},{18,12},{19,13},{20,14},{21,15}} | collective-permute-start | bytes 1572872 | tf_op jit(solution)/shard_map/ppermute | solution.py:517
  4.3 25.1 %collective-permute-start.1 = (f32[8,16,8,128]{3,2,1,0:T(8,128)S(1)}, f32[8,16,8,128]{3,2,1,0:T(8,128)S(1)}, u32[]{:S(2)}, u32[]{:S(2)}) collective-permute-start(f32[8,16,8,128]{3,2,1,0:T(8,128)S(1)} %get-tuple-element.13.block), channel_id=1, source_target_pairs={{73,8},{74,9},{75,10},{76,11},{77,12},{78,13},{79,14},{89,0},{90,1... | collective-permute-start | bytes 1572872 | tf_op jit(solution)/shard_map/ppermute | solution.py:517
  5.1 24.4 %collective-permute-start = (f32[8,16,8,128]{3,2,1,0:T(8,128)S(1)}, f32[8,16,8,128]{3,2,1,0:T(8,128)S(1)}, u32[]{:S(2)}, u32[]{:S(2)}) collective-permute-start(f32[8,16,8,128]{3,2,1,0:T(8,128)S(1)} %get-tuple-element.13.block), channel_id=1, source_target_pairs={{64,9},{65,10},{66,11},{67,12},{68,13},{69,14},{70,15},{80,1},{81,... | collective-permute-start | bytes 1572872 | tf_op jit(solution)/shard_map/ppermute | solution.py:517
  9.2 13.2 %all-to-all-start = ((f32[8,32,128]{2,1,0:T(8,128)}), f32[8,32,128]{2,1,0:T(8,128)S(1)}, u32[]{:S(2)}, u32[]{:S(2)}) async-start(f32[8,32,128]{2,1,0:T(8,128)} %bitcast), calls=%async_computation | async-start | bytes 262144 | tf_op jit(solution)/shard_map/all_to_all | solution.py:523
  22.4 0.7 copy-start.11
  29.4 9.0 %copy-start.6 = (f32[4,10,8,128]{3,2,1,0:T(8,128)}, f32[4,10,8,128]{3,2,1,0:T(8,128)S(1)}, u32[]{:S(2)}) copy-start(f32[4,10,8,128]{3,2,1,0:T(8,128)S(1)} %get-tuple-element.16.fine) | copy-start | bytes 491524
  29.4 9.0 %copy-start.9 = (f32[10,8,128]{2,1,0:T(8,128)}, f32[10,8,128]{2,1,0:T(8,128)S(1)}, u32[]{:S(2)}) copy-start(f32[10,8,128]{2,1,0:T(8,128)S(1)} %get-tuple-element.17.window) | copy-start | bytes 122884
  29.4 9.0 %copy-start.2 = (f32[8,16,8,128]{3,2,1,0:T(8,128)}, f32[8,16,8,128]{3,2,1,0:T(8,128)S(1)}, u32[]{:S(2)}) copy-start(f32[8,16,8,128]{3,2,1,0:T(8,128)S(1)} %collective-permute-done.3.far_right) | copy-start | bytes 1572868
  29.4 8.9 %copy-start.3 = (f32[8,16,8,128]{3,2,1,0:T(8,128)}, f32[8,16,8,128]{3,2,1,0:T(8,128)S(1)}, u32[]{:S(2)}) copy-start(f32[8,16,8,128]{3,2,1,0:T(8,128)S(1)} %collective-permute-done.2.far_left) | copy-start | bytes 1572868
  29.4 8.9 %copy-start.4 = (f32[8,16,8,128]{3,2,1,0:T(8,128)}, f32[8,16,8,128]{3,2,1,0:T(8,128)S(1)}, u32[]{:S(2)}) copy-start(f32[8,16,8,128]{3,2,1,0:T(8,128)S(1)} %collective-permute-done.1.right) | copy-start | bytes 1572868
  29.5 8.9 %copy-start.5 = (f32[8,16,8,128]{3,2,1,0:T(8,128)}, f32[8,16,8,128]{3,2,1,0:T(8,128)S(1)}, u32[]{:S(2)}) copy-start(f32[8,16,8,128]{3,2,1,0:T(8,128)S(1)} %collective-permute-done.left) | copy-start | bytes 1572868
  38.4 23.9 %all-to-all-start.1 = ((f32[128,16,128]{2,1,0:T(8,128)}), f32[128,16,128]{2,1,0:T(8,128)S(1)}, u32[]{:S(2)}, u32[]{:S(2)}) async-start(f32[128,16,128]{2,1,0:T(8,128)} %bitcast.2), calls=%async_computation.1 | async-start | bytes 2097152 | tf_op jit(solution)/shard_map/all_to_all | solution.py:545
  44.1 18.3 %copy-start.7 = (f32[4,10,8,128]{3,2,1,0:T(8,128)S(1)}, f32[4,10,8,128]{3,2,1,0:T(8,128)}, u32[]{:S(2)}) copy-start(f32[4,10,8,128]{3,2,1,0:T(8,128)} %copy-done.6) | copy-start | bytes 491524
  62.3 1.4 %copy-start = (f32[24,16,8,128]{3,2,1,0:T(8,128)S(1)}, f32[24,16,8,128]{3,2,1,0:T(8,128)}, u32[]{:S(2)}) copy-start(f32[24,16,8,128]{3,2,1,0:T(8,128)} %wide_sweeps.1.state) | copy-start | bytes 4718596

commit v3 on v2

--- a/solution.py
+++ b/solution.py
@@ -9,6 +9,7 @@
 FINE_STEPS = 2
 SWEEPS = 8
 C_SWEEPS = 4
+REGIONS = 6
 WINDOW = 40
 NEAR = 16
 OWN = 32
@@ -59,9 +60,8 @@
     return jnp.where(masks[3], 0.0, pltpu.roll(tile, 127, 1))
 
 
-def sweep(source, target, scaled, weight_ref, start, stop, masks, fresh=None):
-    def body(t, carry):
-        base = start + UNROLL * t
+def sweep(source, target, scaled, weight_ref, group, masks, fresh=None):
+    def planes(base, last):
         for u in range(UNROLL):
             i = base + u + 1
             k = lax.shift_right_logical(base + u, 2)
@@ -82,10 +82,17 @@
                 else:
                     term = (cur[p] + heat) * inverse
                     scaled[i, p] = term
-                target[i, p] = term + weight * total
+                value = term + weight * total
+                target[i, p] = value
+                if last and u == UNROLL - 1:
+                    target[WINDOW + 1, p] = swap(value)
+
+    def body(t, carry):
+        planes(UNROLL * t, False)
         return carry
 
-    lax.fori_loop(0, stop, body, 0)
+    lax.fori_loop(group, WINDOW // UNROLL - 1, body, 0)
+    planes(jnp.int32(WINDOW - UNROLL), True)
 
 
 def fold(buffer):
@@ -98,9 +105,7 @@
 
     def one(source, target, q, fresh=None):
         group = lax.div(first + q, UNROLL)
-        steps = WINDOW // UNROLL - group
-        sweep(source, target, scaled, weight_ref, UNROLL * group, steps, masks, fresh)
-        fold(target)
+        sweep(source, target, scaled, weight_ref, group, masks, fresh)
 
     fold(even)
     for step in range(FINE_STEPS):
@@ -194,6 +199,9 @@
 
 
 def difference_chain(received, shift, table_ref, ends, masks, half):
+    def arrived(sender):
+        return blocks_to_global(lambda b, k: received[sender * 8 + b, k], half)
+
     def body(m, delta):
         scaled = [delta[i] * table_ref[0, i] for i in range(16)]
         weight = [table_ref[1, i] for i in range(16)]
@@ -202,12 +210,12 @@
             field = coarse_sweep(field, scaled, weight, masks)
         for i in range(16):
             ends[m, i] = field[i]
-        sender = jnp.minimum(m + shift, 15)
-        added = blocks_to_global(lambda b, k: received[sender * 8 + b, k], half)
+        added = arrived(jnp.minimum(m + shift, 15))
         return tuple(field[i] + added[i] for i in range(16))
 
-    zero = jnp.zeros((8, 128), f32)
-    lax.fori_loop(0, 16, body, (zero,) * 16)
+    for i in range(16):
+        ends[0, i] = jnp.zeros((8, 128), f32)
+    lax.fori_loop(1, 16, body, tuple(arrived(shift)))
 
 
 def split_dot(values, matrix):
@@ -230,7 +238,11 @@
     return jnp.where(hit, 1.0, 0.0).astype(jnp.bfloat16)
 
 
-def to_phases(initial, labels, block, send, narrow, left, right):
+def to_phases(rates, heat, initial, labels, block, send, values, narrow, left, right):
+    for region in range(REGIONS):
+        values[region] = jnp.full((8, 128), rates[region], f32)
+        for m in range(16):
+            values[REGIONS * (m + 1) + region] = jnp.full((8, 128), heat[region, m], f32)
     half = half_mask()
     matrix = interleave_matrix(False)
     for side in range(2):
@@ -272,13 +284,16 @@
     return total
 
 
-def first_chain(rates, heat, received, base, fine, table, window, chain, padded):
+def first_chain(values, received, base, fine, table, window, chain, padded):
     half = half_mask()
     masks = edge_masks()
     index, space = coordinates()
     before = jnp.maximum(index - 1, 0)
-    count = 6
-    rate_values = [rates[r] for r in range(count)]
+    rate_values = [values[r] for r in range(REGIONS)]
+
+    def heat_values(m):
+        return [values[REGIONS * (m + 1) + r] for r in range(REGIONS)]
+
     tags = blocks_to_global(lambda b, k: received[b, 2 + k], half)
     start = blocks_to_global(lambda b, k: received[b, k], half)
     for i in range(16):
@@ -300,14 +315,14 @@
         inverse = jnp.where(tag < 0.0, 0.0, 1.0 / (1.0 + 6.0 * rate))
         fine[0, k] = inverse
         fine[1, k] = rate * inverse
-        fine[2, k] = regions(tag, [heat[before, r] for r in range(count)])
-        fine[3, k] = regions(tag, [heat[index, r] for r in range(count)])
+        fine[2, k] = regions(tag, heat_values(before))
+        fine[3, k] = regions(tag, heat_values(index))
 
     def advance(m, state):
-        values = [FINE_STEPS * heat[m, r] for r in range(count)]
+        heats = [FINE_STEPS * x for x in heat_values(m)]
         weight = [table[1, i] for i in range(16)]
         rows = [
-            (state[i] + regions(table[2, i], values)) * table[0, i] for i in range(16)
+            (state[i] + regions(table[2, i], heats)) * table[0, i] for i in range(16)
         ]
         field = list(state)
         for _ in range(C_SWEEPS):
@@ -502,10 +517,10 @@
     block_shape = (8, 16) + tile
     buffer = (WINDOW + 2, 16) + tile
 
-    block, send = call(
+    block, send, values = call(
         to_phases,
-        [(initial_temp, "near"), (region_labels, "near")],
-        [(block_shape, "near"), ((8, 4) + tile, "near")],
+        [(region_rate, "scalar"), (heat_rate.T, "scalar"), (initial_temp, "near"), (region_labels, "near")],
+        [(block_shape, "near"), ((8, 4) + tile, "near"), ((17 * REGIONS,) + tile, "near")],
         [(2, 512, 128), (512, 256), (512, 256)],
     )
 
@@ -526,7 +541,7 @@
 
     base, fine, table, window = call(
         first_chain,
-        [(region_rate, "scalar"), (heat_rate, "scalar"), (received, "near")],
+        [(values, "near"), (received, "near")],
         [((4,) + tile, "near"), ((4, GROUPS) + tile, "near"), ((3, 16) + tile, "near"),
          ((GROUPS,) + tile, "near")],
         [(17, 16) + tile, (48,) + tile],

time: 110 us -> 107 us (0.973)
  blocking collectives: 24.9 us -> 36.9 us
  waiting for transfers between devices: 10.1 us -> 3.96 us
  starting transfers between devices: 17.2 us -> 12.8 us
  Pallas kernels: 51.7 us -> 47.5 us
    all_to_all x0 -> x1, blocking collectives: none -> 13 us  [on_device(): lax.all_to_all(send.reshape(8 * 32, 128), 'space', 0, 0, tiled=True)]
    all_to_all x1 -> x0, waiting for transfers between devices: 7.15 us -> none  [on_device(): lax.all_to_all(send.reshape(8 * 32, 128), 'space', 0, 0, tiled=True)]
    all_to_all x1 -> x0, starting transfers between devices: 5.32 us -> none  [on_device(): lax.all_to_all(send.reshape(8 * 32, 128), 'space', 0, 0, tiled=True)]
    pallas_call x6, Pallas kernels: 51.7 us -> 47.5 us  [call(): pl.pallas_call(kernel, out_shape=shapes, in_specs=[pl.BlockSpec(memory_sp...]
    unnamed x25 -> x26, local copies, waits for them, and re-layouts: 4.62 us -> 4.54 us
  transfers between devices with their start and end apart: 6 -> 5, of which waited for: 2 -> 1; matrix products, arithmetic and copies ran while one was open for 1% -> 0% of each run, Pallas kernels for 20% -> 19%
where the time goes in v3:
time: 107 us; the launch traced here: 106 us
  Pallas kernels  47.5 us (44%)
  blocking collectives  36.9 us (34%)
  starting transfers between devices  12.8 us (12%)
  local copies, waits for them, and re-layouts  4.54 us (4%)
  waiting for transfers between devices  3.96 us (4%)
    pallas_call x6, Pallas kernels, call(): pl.pallas_call(kernel, out_shape=shapes, in_specs=[pl.BlockSpec(memory_sp...  47.5 us
    all_to_all x1, blocking collectives, gather(): rows = lax.all_to_all(rows, ('tm', 'space'), 0, 0, tiled=True)  23.9 us
    all_to_all x1, blocking collectives, on_device(): lax.all_to_all(send.reshape(8 * 32, 128), 'space', 0, 0, tiled=True)  13 us
    all_to_all x1, starting transfers between devices, gather(): rows = lax.all_to_all(rows, ('tm', 'space'), 0, 0, tiled=True)  6.59 us
    ppermute x4, starting transfers between devices, beside(): return lax.ppermute(block, ('tm', 'space'), pairs)  6.23 us
    unnamed x26, local copies, waits for them, and re-layouts  4.54 us
    all_to_all x1, waiting for transfers between devices, gather(): rows = lax.all_to_all(rows, ('tm', 'space'), 0, 0, tiled=True)  3.95 us
  transfers between devices with their start and end apart: 5, of which 1 were waited for; matrix products, arithmetic and copies ran while one was open for 0% of the time, Pallas kernels for 19%

profile of v3, /device:TPU:8, one launch (start us, length us, event | category | flops | bytes accessed | tf_op | source)
XLA Modules:
  0.0 105.9 jit_solution(10849072158147354781)
XLA Ops:
  0.0 1.0 copy-done.8
  1.0 0.7 copy-done.10
  1.8 0.7 copy-done.11
  2.5 0.7 copy-done.12
  3.1 1.2 %to_phases.1 = (f32[8,16,8,128]{3,2,1,0:T(8,128)S(1)}, f32[8,4,8,128]{3,2,1,0:T(8,128)S(1)}, f32[102,8,128]{2,1,0:T(8,128)S(1)}) custom-call(f32[6]{0:T(128)S(1)} %copy-done.12, f32[6,16]{1,0:T(8,128)S(1)} %bitcast.12, f32[16,32,256]{2,1,0:T(8,128)S(1)} %copy-done.8, s32[4,8,64]{2,1,0:T(8,128)S(1)} %copy-done.10), custom_call_target="tpu_custom_call" | custom-call | bytes 1606040 | tf_op jit(solution)/shard_map/to_phases/pallas_call | solution.py:502
  4.3 0.0 copy-start.1
  4.3 0.7 collective-permute-start.3
  5.0 0.7 collective-permute-start.2
  5.7 0.7 collective-permute-start.1
  6.4 4.1 %collective-permute-start = (f32[8,16,8,128]{3,2,1,0:T(8,128)S(1)}, f32[8,16,8,128]{3,2,1,0:T(8,128)S(1)}, u32[]{:S(2)}, u32[]{:S(2)}) collective-permute-start(f32[8,16,8,128]{3,2,1,0:T(8,128)S(1)} %get-tuple-element.14.block), channel_id=1, source_target_pairs={{64,9},{65,10},{66,11},{67,12},{68,13},{69,14},{70,15},{80,1},{81,... | collective-permute-start | bytes 1572872 | tf_op jit(solution)/shard_map/ppermute | solution.py:532
  10.5 13.0 %all_to_all.27 = f32[8,32,128]{2,1,0:T(8,128)S(1)} all-to-all(f32[8,32,128]{2,1,0:T(8,128)S(1)} %bitcast.11), channel_id=1, replica_groups=mesh['tm'=16,'space'=8] {'space'}, dimensions={0} | all-to-all | bytes 262144 | tf_op jit(solution)/shard_map/all_to_all | solution.py:538
  23.6 5.6 %first_chain.1 = (f32[4,8,128]{2,1,0:T(8,128)S(1)}, f32[4,10,8,128]{3,2,1,0:T(8,128)S(1)}, f32[3,16,8,128]{3,2,1,0:T(8,128)S(1)}, f32[10,8,128]{2,1,0:T(8,128)S(1)}) custom-call(f32[102,8,128]{2,1,0:T(8,128)S(1)} %get-tuple-element.15.values, f32[8,4,8,128]{3,2,1,0:T(8,128)S(1)} %bitcast.10), custom_call_target="tpu_custom_call" | custom-call | bytes 966656 | tf_op jit(solution)/shard_map/first_chain/pallas_call | solution.py:502
  29.2 0.0 collective-permute-done.3.far_right
  29.2 0.0 collective-permute-done.2.far_left
  29.2 0.0 collective-permute-done.1.right
  29.3 0.0 collective-permute-done.left
  29.3 7.8 %first_sweeps.1 = f32[128,2,8,128]{3,2,1,0:T(8,128)} custom-call(f32[8,16,8,128]{3,2,1,0:T(8,128)S(1)} %get-tuple-element.14.block, f32[8,16,8,128]{3,2,1,0:T(8,128)S(1)} %collective-permute-done.left, f32[8,16,8,128]{3,2,1,0:T(8,128)S(1)} %collective-permute-done.1.right, f32[8,16,8,128]{3,2,1,0:T(8,128)S(1)} %collective-permute-done.2.far_left, ...), custom_call_target="tpu_custom_call" | custom-call | bytes 3891200 | tf_op jit(solution)/shard_map/first_sweeps/pallas_call | solution.py:502
  37.2 6.6 %all-to-all-start.1 = ((f32[128,16,128]{2,1,0:T(8,128)}), f32[128,16,128]{2,1,0:T(8,128)S(1)}, u32[]{:S(2)}, u32[]{:S(2)}) async-start(f32[128,16,128]{2,1,0:T(8,128)} %bitcast.3), calls=%async_computation.1 | async-start | bytes 2097152 | tf_op jit(solution)/shard_map/all_to_all | solution.py:560
  43.8 14.3 %wide_sweeps.1.state = f32[24,16,8,128]{3,2,1,0:T(8,128)} custom-call(f32[4,10,8,128]{3,2,1,0:T(8,128)} %copy-done.6, f32[10,8,128]{2,1,0:T(8,128)} %copy-done.9, f32[8,16,8,128]{3,2,1,0:T(8,128)} %copy-done.1, f32[8,16,8,128]{3,2,1,0:T(8,128)} %copy-done.5, f32[8,16,8,128]{3,2,1,0:T(8,128)} %copy-done.4, f32[8,16,8,128]{3,2,1,0:T(8,128)} %copy-done.3, ...), custom_call_target="tpu_custom_call" | custom-call | flops 100000000 | bytes 4399104 | tf_op jit(solution)/shard_map/wide_sweeps/pallas_call | solution.py:502
  58.1 3.9 %all-to-all-done.1 = f32[128,16,128]{2,1,0:T(8,128)S(1)} async-done(((f32[128,16,128]{2,1,0:T(8,128)}), f32[128,16,128]{2,1,0:T(8,128)S(1)}, u32[]{:S(2)}, u32[]{:S(2)}) %all-to-all-start.1) | async-done | bytes 1048608 | tf_op jit(solution)/shard_map/all_to_all | solution.py:560
  62.1 1.4 %copy-done = f32[24,16,8,128]{3,2,1,0:T(8,128)S(1)} copy-done((f32[24,16,8,128]{3,2,1,0:T(8,128)S(1)}, f32[24,16,8,128]{3,2,1,0:T(8,128)}, u32[]{:S(2)}) %copy-start) | copy-done | bytes 1572888
  63.5 12.1 %second_sweeps.1 = (f32[128,2,8,128]{3,2,1,0:T(8,128)S(1)}, f32[8,16,8,128]{3,2,1,0:T(8,128)S(1)}) custom-call(f32[128,2,8,128]{3,2,1,0:T(8,128)S(1)} %bitcast.7, f32[24,16,8,128]{3,2,1,0:T(8,128)S(1)} %copy-done, f32[4,8,128]{2,1,0:T(8,128)S(1)} %get-tuple-element.17.base, f32[4,10,8,128]{3,2,1,0:T(8,128)S(1)} %copy-done.7, ...), custom_call_target="tpu_custom_call" | custom-call | bytes 4571136 | tf_op jit(solution)/shard_map/second_sweeps/pallas_call | solution.py:502
  75.6 23.9 %all_to_all.28 = f32[128,16,128]{2,1,0:T(8,128)S(1)} all-to-all(f32[128,16,128]{2,1,0:T(8,128)S(1)} %bitcast.9), channel_id=1, replica_groups=mesh['tm'=16,'space'=8] {'tm','space'}, dimensions={0} | all-to-all | bytes 2097152 | tf_op jit(solution)/shard_map/all_to_all | solution.py:560
  99.5 6.4 %finish.1 = f32[1,16,32,256]{3,2,1,0:T(8,128)} custom-call(f32[128,2,8,128]{3,2,1,0:T(8,128)S(1)} %bitcast.8, f32[8,16,8,128]{3,2,1,0:T(8,128)S(1)} %get-tuple-element.22.result, f32[3,16,8,128]{3,2,1,0:T(8,128)S(1)} %get-tuple-element.20.table), custom_call_target="tpu_custom_call" | custom-call | bytes 2293760 | tf_op jit(solution)/shard_map/finish/pallas_call | solution.py:502
  (20 shorter events, 0.0 us)
Async XLA Ops:
  0.0 1.0 copy-start.8
  1.0 0.7 copy-start.10
  1.8 0.7 copy-start.11
  2.4 0.7 copy-start.12
  4.3 32.9 %copy-start.1 = (f32[8,16,8,128]{3,2,1,0:T(8,128)}, f32[8,16,8,128]{3,2,1,0:T(8,128)S(1)}, u32[]{:S(2)}) copy-start(f32[8,16,8,128]{3,2,1,0:T(8,128)S(1)} %get-tuple-element.14.block) | copy-start | bytes 1572868
  4.3 24.9 %collective-permute-start.3 = (f32[8,16,8,128]{3,2,1,0:T(8,128)S(1)}, f32[8,16,8,128]{3,2,1,0:T(8,128)S(1)}, u32[]{:S(2)}, u32[]{:S(2)}) collective-permute-start(f32[8,16,8,128]{3,2,1,0:T(8,128)S(1)} %get-tuple-element.14.block), channel_id=1, source_target_pairs={{50,8},{51,9},{52,10},{53,11},{54,12},{55,13}} | collective-permute-start | bytes 1572872 | tf_op jit(solution)/shard_map/ppermute | solution.py:532
  5.0 24.2 %collective-permute-start.2 = (f32[8,16,8,128]{3,2,1,0:T(8,128)S(1)}, f32[8,16,8,128]{3,2,1,0:T(8,128)S(1)}, u32[]{:S(2)}, u32[]{:S(2)}) collective-permute-start(f32[8,16,8,128]{3,2,1,0:T(8,128)S(1)} %get-tuple-element.14.block), channel_id=1, source_target_pairs={{16,10},{17,11},{18,12},{19,13},{20,14},{21,15}} | collective-permute-start | bytes 1572872 | tf_op jit(solution)/shard_map/ppermute | solution.py:532
  5.7 23.6 %collective-permute-start.1 = (f32[8,16,8,128]{3,2,1,0:T(8,128)S(1)}, f32[8,16,8,128]{3,2,1,0:T(8,128)S(1)}, u32[]{:S(2)}, u32[]{:S(2)}) collective-permute-start(f32[8,16,8,128]{3,2,1,0:T(8,128)S(1)} %get-tuple-element.14.block), channel_id=1, source_target_pairs={{73,8},{74,9},{75,10},{76,11},{77,12},{78,13},{79,14},{89,0},{90,1... | collective-permute-start | bytes 1572872 | tf_op jit(solution)/shard_map/ppermute | solution.py:532
  6.4 22.9 %collective-permute-start = (f32[8,16,8,128]{3,2,1,0:T(8,128)S(1)}, f32[8,16,8,128]{3,2,1,0:T(8,128)S(1)}, u32[]{:S(2)}, u32[]{:S(2)}) collective-permute-start(f32[8,16,8,128]{3,2,1,0:T(8,128)S(1)} %get-tuple-element.14.block), channel_id=1, source_target_pairs={{64,9},{65,10},{66,11},{67,12},{68,13},{69,14},{70,15},{80,1},{81,... | collective-permute-start | bytes 1572872 | tf_op jit(solution)/shard_map/ppermute | solution.py:532
  29.2 8.0 %copy-start.6 = (f32[4,10,8,128]{3,2,1,0:T(8,128)}, f32[4,10,8,128]{3,2,1,0:T(8,128)S(1)}, u32[]{:S(2)}) copy-start(f32[4,10,8,128]{3,2,1,0:T(8,128)S(1)} %get-tuple-element.18.fine) | copy-start | bytes 491524
  29.2 8.0 %copy-start.9 = (f32[10,8,128]{2,1,0:T(8,128)}, f32[10,8,128]{2,1,0:T(8,128)S(1)}, u32[]{:S(2)}) copy-start(f32[10,8,128]{2,1,0:T(8,128)S(1)} %get-tuple-element.19.window) | copy-start | bytes 122884
  29.2 7.9 %copy-start.2 = (f32[8,16,8,128]{3,2,1,0:T(8,128)}, f32[8,16,8,128]{3,2,1,0:T(8,128)S(1)}, u32[]{:S(2)}) copy-start(f32[8,16,8,128]{3,2,1,0:T(8,128)S(1)} %collective-permute-done.3.far_right) | copy-start | bytes 1572868
  29.2 7.9 %copy-start.3 = (f32[8,16,8,128]{3,2,1,0:T(8,128)}, f32[8,16,8,128]{3,2,1,0:T(8,128)S(1)}, u32[]{:S(2)}) copy-start(f32[8,16,8,128]{3,2,1,0:T(8,128)S(1)} %collective-permute-done.2.far_left) | copy-start | bytes 1572868
  29.3 7.9 %copy-start.4 = (f32[8,16,8,128]{3,2,1,0:T(8,128)}, f32[8,16,8,128]{3,2,1,0:T(8,128)S(1)}, u32[]{:S(2)}) copy-start(f32[8,16,8,128]{3,2,1,0:T(8,128)S(1)} %collective-permute-done.1.right) | copy-start | bytes 1572868
  29.3 7.9 %copy-start.5 = (f32[8,16,8,128]{3,2,1,0:T(8,128)}, f32[8,16,8,128]{3,2,1,0:T(8,128)S(1)}, u32[]{:S(2)}) copy-start(f32[8,16,8,128]{3,2,1,0:T(8,128)S(1)} %collective-permute-done.left) | copy-start | bytes 1572868
  37.2 24.9 %all-to-all-start.1 = ((f32[128,16,128]{2,1,0:T(8,128)}), f32[128,16,128]{2,1,0:T(8,128)S(1)}, u32[]{:S(2)}, u32[]{:S(2)}) async-start(f32[128,16,128]{2,1,0:T(8,128)} %bitcast.3), calls=%async_computation.1 | async-start | bytes 2097152 | tf_op jit(solution)/shard_map/all_to_all | solution.py:560
  43.8 18.3 %copy-start.7 = (f32[4,10,8,128]{3,2,1,0:T(8,128)S(1)}, f32[4,10,8,128]{3,2,1,0:T(8,128)}, u32[]{:S(2)}) copy-start(f32[4,10,8,128]{3,2,1,0:T(8,128)} %copy-done.6) | copy-start | bytes 491524
  62.1 1.4 %copy-start = (f32[24,16,8,128]{3,2,1,0:T(8,128)S(1)}, f32[24,16,8,128]{3,2,1,0:T(8,128)}, u32[]{:S(2)}) copy-start(f32[24,16,8,128]{3,2,1,0:T(8,128)} %wide_sweeps.1.state) | copy-start | bytes 4718596

commit v4 on v3

--- a/solution.py
+++ b/solution.py
@@ -238,11 +238,7 @@
     return jnp.where(hit, 1.0, 0.0).astype(jnp.bfloat16)
 
 
-def to_phases(rates, heat, initial, labels, block, send, values, narrow, left, right):
-    for region in range(REGIONS):
-        values[region] = jnp.full((8, 128), rates[region], f32)
-        for m in range(16):
-            values[REGIONS * (m + 1) + region] = jnp.full((8, 128), heat[region, m], f32)
+def to_phases(initial, labels, block, send, narrow, left, right):
     half = half_mask()
     matrix = interleave_matrix(False)
     for side in range(2):
@@ -517,10 +513,10 @@
     block_shape = (8, 16) + tile
     buffer = (WINDOW + 2, 16) + tile
 
-    block, send, values = call(
+    block, send = call(
         to_phases,
-        [(region_rate, "scalar"), (heat_rate.T, "scalar"), (initial_temp, "near"), (region_labels, "near")],
-        [(block_shape, "near"), ((8, 4) + tile, "near"), ((17 * REGIONS,) + tile, "near")],
+        [(initial_temp, "near"), (region_labels, "near")],
+        [(block_shape, "near"), ((8, 4) + tile, "near")],
         [(2, 512, 128), (512, 256), (512, 256)],
     )
 
@@ -539,6 +535,8 @@
         send.reshape(8 * 32, 128), "space", 0, 0, tiled=True
     ).reshape((8, 4) + tile)
 
+    rows = jnp.concatenate([region_rate, heat_rate.reshape(-1)])
+    values = jnp.broadcast_to(rows[:, None, None], (17 * REGIONS,) + tile)
     base, fine, table, window = call(
         first_chain,
         [(values, "near"), (received, "near")],

time: 107 us -> 106 us (level)
  blocking collectives: 36.9 us -> 23.9 us
  waiting for transfers between devices: 3.96 us -> 10.3 us
  starting transfers between devices: 12.8 us -> 17.8 us
    all_to_all x1 -> x0, blocking collectives: 13 us -> none  [on_device(): lax.all_to_all(send.reshape(8 * 32, 128), 'space', 0, 0, tiled=True)]
    all_to_all x0 -> x1, waiting for transfers between devices: none -> 6.32 us  [on_device(): lax.all_to_all(send.reshape(8 * 32, 128), 'space', 0, 0, tiled=True)]
    all_to_all x0 -> x1, starting transfers between devices: none -> 5.32 us  [on_device(): lax.all_to_all(send.reshape(8 * 32, 128), 'space', 0, 0, tiled=True)]
    unnamed x26 -> x23, local copies, waits for them, and re-layouts: 4.54 us -> 3.96 us
  transfers between devices with their start and end apart: 5 -> 6, of which waited for: 1 -> 2; matrix products, arithmetic and copies ran while one was open for 0% -> 2% of each run, Pallas kernels for 19% -> 19%
where the time goes in v4:
time: 106 us; the launch traced here: 105 us
  Pallas kernels  47.5 us (45%)
  blocking collectives  23.9 us (23%)
  starting transfers between devices  17.8 us (17%)
  waiting for transfers between devices  10.3 us (10%)
  local copies, waits for them, and re-layouts  4.21 us (4%)
    pallas_call x6, Pallas kernels, call(): pl.pallas_call(kernel, out_shape=shapes, in_specs=[pl.BlockSpec(memory_sp...  47.5 us
    all_to_all x1, blocking collectives, gather(): rows = lax.all_to_all(rows, ('tm', 'space'), 0, 0, tiled=True)  23.9 us
    all_to_all x1, waiting for transfers between devices, on_device(): lax.all_to_all(send.reshape(8 * 32, 128), 'space', 0, 0, tiled=True)  6.32 us
    ppermute x4, starting transfers between devices, beside(): return lax.ppermute(block, ('tm', 'space'), pairs)  6.22 us
    all_to_all x1, starting transfers between devices, gather(): rows = lax.all_to_all(rows, ('tm', 'space'), 0, 0, tiled=True)  6.21 us
    all_to_all x1, starting transfers between devices, on_device(): lax.all_to_all(send.reshape(8 * 32, 128), 'space', 0, 0, tiled=True)  5.32 us
    unnamed x23, local copies, waits for them, and re-layouts  3.96 us
    all_to_all x1, waiting for transfers between devices, gather(): rows = lax.all_to_all(rows, ('tm', 'space'), 0, 0, tiled=True)  3.95 us
  transfers between devices with their start and end apart: 6, of which 2 were waited for; matrix products, arithmetic and copies ran while one was open for 2% of the time, Pallas kernels for 19%

profile of v4, /device:TPU:8, one launch (start us, length us, event | category | flops | bytes accessed | tf_op | source)
XLA Modules:
  0.0 104.6 jit_solution(9853302667146789456)
XLA Ops:
  0.0 1.0 copy-done.8
  1.0 0.7 copy-done.10
  1.8 1.2 %to_phases.1 = (f32[8,16,8,128]{3,2,1,0:T(8,128)S(1)}, f32[8,4,8,128]{3,2,1,0:T(8,128)}) custom-call(f32[16,32,256]{2,1,0:T(8,128)S(1)} %copy-done.8, s32[4,8,64]{2,1,0:T(8,128)S(1)} %copy-done.10), custom_call_target="tpu_custom_call" | custom-call | bytes 1187840 | tf_op jit(solution)/shard_map/to_phases/pallas_call | solution.py:498
  3.0 0.7 collective-permute-start.3
  3.6 0.7 collective-permute-start.2
  4.3 0.7 collective-permute-start.1
  5.0 4.1 %collective-permute-start = (f32[8,16,8,128]{3,2,1,0:T(8,128)S(1)}, f32[8,16,8,128]{3,2,1,0:T(8,128)S(1)}, u32[]{:S(2)}, u32[]{:S(2)}) collective-permute-start(f32[8,16,8,128]{3,2,1,0:T(8,128)S(1)} %get-tuple-element.13.block), channel_id=1, source_target_pairs={{64,9},{65,10},{66,11},{67,12},{68,13},{69,14},{70,15},{80,1},{81,... | collective-permute-start | bytes 1572872 | tf_op jit(solution)/shard_map/ppermute | solution.py:528
  9.2 5.3 %all-to-all-start = ((f32[8,32,128]{2,1,0:T(8,128)}), f32[8,32,128]{2,1,0:T(8,128)S(1)}, u32[]{:S(2)}, u32[]{:S(2)}) async-start(f32[8,32,128]{2,1,0:T(8,128)} %bitcast), calls=%async_computation | async-start | bytes 262144 | tf_op jit(solution)/shard_map/all_to_all | solution.py:534
  14.5 0.8 copy.6
  15.3 0.1 reshape.28
  15.4 0.7 pad_maximum_fusion
  16.1 6.3 %all-to-all-done = f32[8,32,128]{2,1,0:T(8,128)S(1)} async-done(((f32[8,32,128]{2,1,0:T(8,128)}), f32[8,32,128]{2,1,0:T(8,128)S(1)}, u32[]{:S(2)}, u32[]{:S(2)}) %all-to-all-start) | async-done | bytes 131104 | tf_op jit(solution)/shard_map/all_to_all | solution.py:534
  22.4 0.2 broadcast_in_dim.2.values
  22.6 5.6 %first_chain.1 = (f32[4,8,128]{2,1,0:T(8,128)S(1)}, f32[4,10,8,128]{3,2,1,0:T(8,128)S(1)}, f32[3,16,8,128]{3,2,1,0:T(8,128)S(1)}, f32[10,8,128]{2,1,0:T(8,128)S(1)}) custom-call(f32[102,8,128]{2,1,0:T(8,128)S(1)} %broadcast_in_dim.2.values, f32[8,4,8,128]{3,2,1,0:T(8,128)S(1)} %bitcast.9), custom_call_target="tpu_custom_call" | custom-call | bytes 966656 | tf_op jit(solution)/shard_map/first_chain/pallas_call | solution.py:498
  28.3 0.0 collective-permute-done.2.far_left
  28.3 0.0 collective-permute-done.1.right
  28.3 7.8 %first_sweeps.1 = f32[128,2,8,128]{3,2,1,0:T(8,128)} custom-call(f32[8,16,8,128]{3,2,1,0:T(8,128)S(1)} %get-tuple-element.13.block, f32[8,16,8,128]{3,2,1,0:T(8,128)S(1)} %collective-permute-done.left, f32[8,16,8,128]{3,2,1,0:T(8,128)S(1)} %collective-permute-done.1.right, f32[8,16,8,128]{3,2,1,0:T(8,128)S(1)} %collective-permute-done.2.far_left, ...), custom_call_target="tpu_custom_call" | custom-call | bytes 3891200 | tf_op jit(solution)/shard_map/first_sweeps/pallas_call | solution.py:498
  36.2 6.2 %all-to-all-start.1 = ((f32[128,16,128]{2,1,0:T(8,128)}), f32[128,16,128]{2,1,0:T(8,128)S(1)}, u32[]{:S(2)}, u32[]{:S(2)}) async-start(f32[128,16,128]{2,1,0:T(8,128)} %bitcast.2), calls=%async_computation.1 | async-start | bytes 2097152 | tf_op jit(solution)/shard_map/all_to_all | solution.py:558
  42.5 14.3 %wide_sweeps.1.state = f32[24,16,8,128]{3,2,1,0:T(8,128)} custom-call(f32[4,10,8,128]{3,2,1,0:T(8,128)} %copy-done.6, f32[10,8,128]{2,1,0:T(8,128)} %copy-done.9, f32[8,16,8,128]{3,2,1,0:T(8,128)} %copy-done.1, f32[8,16,8,128]{3,2,1,0:T(8,128)} %copy-done.5, f32[8,16,8,128]{3,2,1,0:T(8,128)} %copy-done.4, f32[8,16,8,128]{3,2,1,0:T(8,128)} %copy-done.3, ...), custom_call_target="tpu_custom_call" | custom-call | flops 100000000 | bytes 4399104 | tf_op jit(solution)/shard_map/wide_sweeps/pallas_call | solution.py:498
  56.8 3.9 %all-to-all-done.1 = f32[128,16,128]{2,1,0:T(8,128)S(1)} async-done(((f32[128,16,128]{2,1,0:T(8,128)}), f32[128,16,128]{2,1,0:T(8,128)S(1)}, u32[]{:S(2)}, u32[]{:S(2)}) %all-to-all-start.1) | async-done | bytes 1048608 | tf_op jit(solution)/shard_map/all_to_all | solution.py:558
  60.7 1.4 %copy-done = f32[24,16,8,128]{3,2,1,0:T(8,128)S(1)} copy-done((f32[24,16,8,128]{3,2,1,0:T(8,128)S(1)}, f32[24,16,8,128]{3,2,1,0:T(8,128)}, u32[]{:S(2)}) %copy-start) | copy-done | bytes 1572888
  62.1 12.1 %second_sweeps.1 = (f32[128,2,8,128]{3,2,1,0:T(8,128)S(1)}, f32[8,16,8,128]{3,2,1,0:T(8,128)S(1)}) custom-call(f32[128,2,8,128]{3,2,1,0:T(8,128)S(1)} %bitcast.6, f32[24,16,8,128]{3,2,1,0:T(8,128)S(1)} %copy-done, f32[4,8,128]{2,1,0:T(8,128)S(1)} %get-tuple-element.15.base, f32[4,10,8,128]{3,2,1,0:T(8,128)S(1)} %copy-done.7, ...), custom_call_target="tpu_custom_call" | custom-call | bytes 4571136 | tf_op jit(solution)/shard_map/second_sweeps/pallas_call | solution.py:498
  74.3 23.9 %all_to_all.27 = f32[128,16,128]{2,1,0:T(8,128)S(1)} all-to-all(f32[128,16,128]{2,1,0:T(8,128)S(1)} %bitcast.8), channel_id=1, replica_groups=mesh['tm'=16,'space'=8] {'tm','space'}, dimensions={0} | all-to-all | bytes 2097152 | tf_op jit(solution)/shard_map/all_to_all | solution.py:558
  98.2 6.4 %finish.1 = f32[1,16,32,256]{3,2,1,0:T(8,128)} custom-call(f32[128,2,8,128]{3,2,1,0:T(8,128)S(1)} %bitcast.7, f32[8,16,8,128]{3,2,1,0:T(8,128)S(1)} %get-tuple-element.20.result, f32[3,16,8,128]{3,2,1,0:T(8,128)S(1)} %get-tuple-element.18.table), custom_call_target="tpu_custom_call" | custom-call | bytes 2293760 | tf_op jit(solution)/shard_map/finish/pallas_call | solution.py:498
  (21 shorter events, 0.0 us)
Async XLA Ops:
  0.0 1.0 copy-start.8
  1.0 0.7 copy-start.10
  2.9 33.2 %copy-start.1 = (f32[8,16,8,128]{3,2,1,0:T(8,128)}, f32[8,16,8,128]{3,2,1,0:T(8,128)S(1)}, u32[]{:S(2)}) copy-start(f32[8,16,8,128]{3,2,1,0:T(8,128)S(1)} %get-tuple-element.13.block) | copy-start | bytes 1572868
  3.0 25.3 %collective-permute-start.3 = (f32[8,16,8,128]{3,2,1,0:T(8,128)S(1)}, f32[8,16,8,128]{3,2,1,0:T(8,128)S(1)}, u32[]{:S(2)}, u32[]{:S(2)}) collective-permute-start(f32[8,16,8,128]{3,2,1,0:T(8,128)S(1)} %get-tuple-element.13.block), channel_id=1, source_target_pairs={{50,8},{51,9},{52,10},{53,11},{54,12},{55,13}} | collective-permute-start | bytes 1572872 | tf_op jit(solution)/shard_map/ppermute | solution.py:528
  3.6 24.6 %collective-permute-start.2 = (f32[8,16,8,128]{3,2,1,0:T(8,128)S(1)}, f32[8,16,8,128]{3,2,1,0:T(8,128)S(1)}, u32[]{:S(2)}, u32[]{:S(2)}) collective-permute-start(f32[8,16,8,128]{3,2,1,0:T(8,128)S(1)} %get-tuple-element.13.block), channel_id=1, source_target_pairs={{16,10},{17,11},{18,12},{19,13},{20,14},{21,15}} | collective-permute-start | bytes 1572872 | tf_op jit(solution)/shard_map/ppermute | solution.py:528
  4.3 24.0 %collective-permute-start.1 = (f32[8,16,8,128]{3,2,1,0:T(8,128)S(1)}, f32[8,16,8,128]{3,2,1,0:T(8,128)S(1)}, u32[]{:S(2)}, u32[]{:S(2)}) collective-permute-start(f32[8,16,8,128]{3,2,1,0:T(8,128)S(1)} %get-tuple-element.13.block), channel_id=1, source_target_pairs={{73,8},{74,9},{75,10},{76,11},{77,12},{78,13},{79,14},{89,0},{90,1... | collective-permute-start | bytes 1572872 | tf_op jit(solution)/shard_map/ppermute | solution.py:528
  5.0 23.3 %collective-permute-start = (f32[8,16,8,128]{3,2,1,0:T(8,128)S(1)}, f32[8,16,8,128]{3,2,1,0:T(8,128)S(1)}, u32[]{:S(2)}, u32[]{:S(2)}) collective-permute-start(f32[8,16,8,128]{3,2,1,0:T(8,128)S(1)} %get-tuple-element.13.block), channel_id=1, source_target_pairs={{64,9},{65,10},{66,11},{67,12},{68,13},{69,14},{70,15},{80,1},{81,... | collective-permute-start | bytes 1572872 | tf_op jit(solution)/shard_map/ppermute | solution.py:528
  9.2 13.2 %all-to-all-start = ((f32[8,32,128]{2,1,0:T(8,128)}), f32[8,32,128]{2,1,0:T(8,128)S(1)}, u32[]{:S(2)}, u32[]{:S(2)}) async-start(f32[8,32,128]{2,1,0:T(8,128)} %bitcast), calls=%async_computation | async-start | bytes 262144 | tf_op jit(solution)/shard_map/all_to_all | solution.py:534
  28.2 8.0 %copy-start.6 = (f32[4,10,8,128]{3,2,1,0:T(8,128)}, f32[4,10,8,128]{3,2,1,0:T(8,128)S(1)}, u32[]{:S(2)}) copy-start(f32[4,10,8,128]{3,2,1,0:T(8,128)S(1)} %get-tuple-element.16.fine) | copy-start | bytes 491524
  28.2 8.0 %copy-start.9 = (f32[10,8,128]{2,1,0:T(8,128)}, f32[10,8,128]{2,1,0:T(8,128)S(1)}, u32[]{:S(2)}) copy-start(f32[10,8,128]{2,1,0:T(8,128)S(1)} %get-tuple-element.17.window) | copy-start | bytes 122884
  28.3 7.9 %copy-start.2 = (f32[8,16,8,128]{3,2,1,0:T(8,128)}, f32[8,16,8,128]{3,2,1,0:T(8,128)S(1)}, u32[]{:S(2)}) copy-start(f32[8,16,8,128]{3,2,1,0:T(8,128)S(1)} %collective-permute-done.3.far_right) | copy-start | bytes 1572868
  28.3 7.9 %copy-start.3 = (f32[8,16,8,128]{3,2,1,0:T(8,128)}, f32[8,16,8,128]{3,2,1,0:T(8,128)S(1)}, u32[]{:S(2)}) copy-start(f32[8,16,8,128]{3,2,1,0:T(8,128)S(1)} %collective-permute-done.2.far_left) | copy-start | bytes 1572868
  28.3 7.9 %copy-start.4 = (f32[8,16,8,128]{3,2,1,0:T(8,128)}, f32[8,16,8,128]{3,2,1,0:T(8,128)S(1)}, u32[]{:S(2)}) copy-start(f32[8,16,8,128]{3,2,1,0:T(8,128)S(1)} %collective-permute-done.1.right) | copy-start | bytes 1572868
  28.3 7.9 %copy-start.5 = (f32[8,16,8,128]{3,2,1,0:T(8,128)}, f32[8,16,8,128]{3,2,1,0:T(8,128)S(1)}, u32[]{:S(2)}) copy-start(f32[8,16,8,128]{3,2,1,0:T(8,128)S(1)} %collective-permute-done.left) | copy-start | bytes 1572868
  36.2 24.5 %all-to-all-start.1 = ((f32[128,16,128]{2,1,0:T(8,128)}), f32[128,16,128]{2,1,0:T(8,128)S(1)}, u32[]{:S(2)}, u32[]{:S(2)}) async-start(f32[128,16,128]{2,1,0:T(8,128)} %bitcast.2), calls=%async_computation.1 | async-start | bytes 2097152 | tf_op jit(solution)/shard_map/all_to_all | solution.py:558
  42.5 18.3 %copy-start.7 = (f32[4,10,8,128]{3,2,1,0:T(8,128)S(1)}, f32[4,10,8,128]{3,2,1,0:T(8,128)}, u32[]{:S(2)}) copy-start(f32[4,10,8,128]{3,2,1,0:T(8,128)} %copy-done.6) | copy-start | bytes 491524
  60.7 1.4 %copy-start = (f32[24,16,8,128]{3,2,1,0:T(8,128)S(1)}, f32[24,16,8,128]{3,2,1,0:T(8,128)}, u32[]{:S(2)}) copy-start(f32[24,16,8,128]{3,2,1,0:T(8,128)} %wide_sweeps.1.state) | copy-start | bytes 4718596
